TPU v7x, 256 devices: a whole 4x4x8 slice. The times are simulated.
256 devices in a mesh: own: 64 (over x, z, core), col: 4 (over y).
Axes of the slice: x: 4, y: 4, z: 8, core: 2. Of those that a mesh axis runs over, the one named last changes fastest.
Arguments:
- anc_store: float32 [128, 512, 512], P('own', None, 'col'), may hold values from -6 to 6
- block_map: int32 [128], replicated, may hold values from 0 to 127, as said below
- anc_refs: int32 [128, 3, 3], replicated, may hold values from 0 to 127, as said below
- factor1: bfloat16 [128, 3, 512, 512], P('own', None, 'col'), may hold values from -0.15625 to 0.15625
- dinv1: float32 [128, 512, 512], P('own', 'col'), may hold values from -6 to 6
- factor2: bfloat16 [128, 3, 512, 512], P('own', None, 'col'), may hold values from -0.15625 to 0.15625
- dinv2: float32 [128, 512, 512], P('own', 'col'), may hold values from -6 to 6
- parent: int32 [128], P('own'), may hold values from 0 to 1
- picked: int32 [128, 2], P('own'), may hold values from 0 to 2, as said below
Outputs:
- cross1: float32 [128, 3, 512, 512], P('own', None, 'col')
- diag1: float32 [128, 512, 512], P('own', 'col')
- cross2: float32 [128, 3, 512, 512], P('own', None, 'col')
- diag2: float32 [128, 512, 512], P('own', 'col')
Inputs may be any that keep to these rules, and one draw needn't show every extreme that they name: A permutation: tile t is held by owner block_map[t] // 2 in its slot block_map[t] % 2. `anc_refs`: the 18 references of one owner's level-1 blocks name tiles held by any single owner at most 1 times, and exactly 1 times for some owner. `picked`: entries of one row are distinct.
All inputs are finite; a program needn't handle non-finite values.
Results may differ from a plain program's by a relative error of at most 0.0036.
Values may be sent and summed in bfloat16 or wider, within the bound.
A program may use at most 64 MiB of HBM per device.

v0:
```python
import jax
import jax.numpy as jnp
from jax import lax
from jax.sharding import PartitionSpec as P


def fetch_tiles(store_low, positions, held, blocks_here):
    owner_total = lax.axis_size("own")
    my_index = lax.axis_index("own")
    depth = positions.shape[1]
    width = store_low.shape[1]
    narrow = store_low.shape[2]
    request_total = blocks_here * depth * depth
    owner_of = (positions // held).reshape(owner_total, request_total)
    slot_of = (positions % held).reshape(owner_total, request_total)
    earlier = jnp.arange(request_total)[None, :] < jnp.arange(request_total)[:, None]
    same_owner = owner_of[:, :, None] == owner_of[:, None, :]
    slot_rank = jnp.sum((same_owner & earlier[None]).astype(jnp.int32), axis=2)
    capacity = -(-request_total // owner_total)
    chosen = (owner_of == my_index)[:, :, None] & (
        slot_rank[:, :, None] == jnp.arange(capacity)[None, None, :]
    )
    send_slot = jnp.sum(jnp.where(chosen, slot_of[:, :, None], 0), axis=1)
    outgoing = store_low[send_slot.reshape(-1)].reshape(owner_total, capacity, width, narrow)
    incoming = lax.all_to_all(outgoing, "own", split_axis=0, concat_axis=0, tiled=True)
    my_owners = lax.dynamic_index_in_dim(owner_of, my_index, 0, keepdims=False)
    my_ranks = lax.dynamic_index_in_dim(slot_rank, my_index, 0, keepdims=False)
    flattened = incoming.reshape(owner_total * capacity, width, narrow)
    return flattened[my_owners * capacity + my_ranks].reshape(
        blocks_here, depth, depth, width, narrow
    )


def solve_level(tiles, factor, dinv):
    blocks_here, depth, _, width, narrow = tiles.shape
    unit_rows = blocks_here * depth * narrow
    negated = -factor
    groups = unit_rows * lax.axis_size("col") // unit_rows
    row_part = tiles
    row_part = row_part.reshape(blocks_here, depth, depth, groups, narrow, narrow)
    product = jnp.einsum(
        "mikgrp,mkpj->gmirj", row_part, negated, preferred_element_type=jnp.float32
    )
    cross = lax.psum_scatter(
        product.reshape(groups * unit_rows, width), "col", scatter_dimension=0, tiled=True
    ).reshape(blocks_here, depth, narrow, width)
    cross_low = cross.astype(jnp.bfloat16)
    partial_diag = jnp.einsum(
        "mkpj,mkpl->mjl", factor, cross_low, preferred_element_type=jnp.float32
    )
    diag_block = dinv - lax.psum_scatter(partial_diag, "col", scatter_dimension=1, tiled=True)
    return (cross, cross_low, diag_block)


def assemble(parent_rows, parent_cols, diag_rows, parent_tiles, choose):
    corner = diag_rows.T
    top_row = jnp.concatenate([corner[None], jnp.swapaxes(parent_rows[choose], 1, 2)], 0)
    left_col = parent_cols[choose]
    inner_tiles = parent_tiles[choose][:, choose]
    lower_rows = jnp.concatenate([left_col[:, None], inner_tiles], 1)
    return jnp.concatenate([top_row[None], lower_rows], 0)


def per_device(anc_store, block_map, anc_refs, factor1, dinv1, factor2, dinv2, parent, picked):
    held = anc_store.shape[0]
    blocks_here = factor1.shape[0]
    store_low = anc_store.astype(jnp.bfloat16)
    positions = block_map[anc_refs]
    tiles1 = fetch_tiles(store_low, positions, held, blocks_here)
    cross1, cross_low1, diag1 = solve_level(tiles1, factor1, dinv1)
    columns1 = lax.all_to_all(cross_low1, "col", split_axis=3, concat_axis=2, tiled=True)
    diag_low1 = diag1.astype(jnp.bfloat16)
    tiles2 = jax.vmap(assemble)(
        cross_low1[parent], columns1[parent], diag_low1[parent], tiles1[parent], picked
    )
    cross2, cross_low2, diag2 = solve_level(tiles2, factor2, dinv2)
    return (cross1, diag1, cross2, diag2)


def solution(mesh):
    return jax.shard_map(
        per_device,
        mesh=mesh,
        in_specs=(
            P("own", None, "col"),
            P(),
            P(),
            P("own", None, "col", None),
            P("own", "col", None),
            P("own", None, "col", None),
            P("own", "col", None),
            P("own"),
            P("own", None),
        ),
        out_specs=(
            P("own", None, "col", None),
            P("own", "col", None),
            P("own", None, "col", None),
            P("own", "col", None),
        ),
        check_vma=False,
    )
```

profile of v0, /device:TPU:1, one launch (start us, length us, event | category | flops | bytes accessed | tf_op | source)
XLA Modules:
  0.0 454.3 jit_solution(16913347559435713881)
XLA Ops:
  7.2 0.7 compare_select_fusion
  8.3 7.0 %gather_fusion = s32[1152]{0:T(1024)S(1)} fusion(s32[128]{0:T(128)S(1)} %copy-done, s32[2048]{0:T(1024)S(1)} %pad_clamp_fusion), kind=kCustom, calls=%fused_computation | custom fusion | bytes 13824 | tf_op jit(solution)/shard_map/gather | solution.py:68
  16.9 5.3 %gather_fusion.1 = bf16[64,512,128]{2,1,0:T(8,128)(2,1)} fusion(bf16[2,512,128]{2,1,0:T(8,128)(2,1)S(1)} %convert_element_type.15, s32[1024]{0:T(1024)S(1)} %pad_clamp_fusion.3), kind=kCustom, calls=%fused_computation.1 | custom fusion | bytes 16777472 | tf_op jit(solution)/shard_map/gather | solution.py:24
  22.2 13.2 %all-to-all-start = ((bf16[64,1,512,128]{3,2,1,0:T(8,128)(2,1)}), bf16[64,1,512,128]{3,2,1,0:T(8,128)(2,1)}, u32[]{:S(2)}, u32[]{:S(2)}) async-start(bf16[64,1,512,128]{3,2,1,0:T(8,128)(2,1)} %bitcast.80), calls=%async_computation | async-start | bytes 16777216 | tf_op jit(solution)/shard_map/all_to_all | solution.py:25
  35.6 185.5 %all-to-all-done = bf16[64,1,512,128]{3,2,1,0:T(8,128)(2,1)} async-done(((bf16[64,1,512,128]{3,2,1,0:T(8,128)(2,1)}), bf16[64,1,512,128]{3,2,1,0:T(8,128)(2,1)}, u32[]{:S(2)}, u32[]{:S(2)}) %all-to-all-start) | async-done | bytes 8388640 | tf_op jit(solution)/shard_map/all_to_all | solution.py:25
  221.1 4.5 gather_fusion.2
  225.6 1.8 convolution_bitcast_fusion
  227.4 3.4 copy.212
  230.8 63.4 %reduce-scatter.5.cloned.1.call-done = f32[768,512]{1,0:T(8,128)} async-done(((f32[3072,512]{1,0:T(8,128)}), f32[768,512]{1,0:T(8,128)}) %reduce-scatter.5.cloned.1.call-update) | async-done | bytes 1572880 | tf_op jit(solution)/shard_map/reduce_scatter | solution.py:44
  294.2 1.5 convert_element_type.17
  295.7 3.2 convolution_bitcast_fusion.3
  299.0 1.9 copy.218
  300.9 4.2 all-to-all-start.1
  305.4 2.0 copy.214
  307.5 2.3 gather_fusion.6
  309.7 2.7 gather_fusion.9
  312.5 1.7 gather_fusion.10
  315.3 1.0 copy.215
  316.3 3.6 all-to-all-done.1
  319.9 1.2 copy.219
  321.6 0.7 gather_fusion.5
  322.3 1.4 gather_fusion.8
  323.7 11.8 %reduce-scatter.7.cloned.1.call-done = f32[2,128,512]{1,2,0:T(8,128)} async-done(((f32[2,512,512]{1,2,0:T(8,128)}), f32[2,128,512]{1,2,0:T(8,128)}) %reduce-scatter.7.cloned.1.call-update) | async-done | bytes 524304 | tf_op jit(solution)/shard_map/reduce_scatter | solution.py:51
  335.5 1.2 fusion.25
  337.3 3.0 convolution_bitcast_fusion.1
  340.3 3.4 copy.223
  343.8 66.2 %reduce-scatter.9.cloned.1.call-done = f32[768,512]{1,0:T(8,128)} async-done(((f32[3072,512]{1,0:T(8,128)}), f32[768,512]{1,0:T(8,128)}) %reduce-scatter.9.cloned.1.call-update) | async-done | bytes 1572880 | tf_op jit(solution)/shard_map/reduce_scatter | solution.py:44
  409.9 3.6 convolution_bitcast_fusion.2
  413.7 1.0 copy.226
  414.7 30.9 %reduce-scatter.11.cloned.1.call-done = f32[2,128,512]{1,2,0:T(8,128)} async-done(((f32[2,512,512]{1,2,0:T(8,128)}), f32[2,128,512]{1,2,0:T(8,128)}) %reduce-scatter.11.cloned.1.call-update) | async-done | bytes 524304 | tf_op jit(solution)/shard_map/reduce_scatter | solution.py:51
  445.7 1.1 sub.17
  446.8 1.0 copy.227
  (60 shorter events, 5.0 us)
Async XLA Ops:
  7.2 1.1 copy-start
  8.3 8.5 %copy-start.6 = (f32[2,512,128]{2,1,0:T(8,128)S(1)}, f32[2,512,128]{2,1,0:T(8,128)}, u32[]{:S(2)}) copy-start(f32[2,512,128]{2,1,0:T(8,128)} %param.9) | copy-start | bytes 1572868
  22.2 198.9 %all-to-all-start = ((bf16[64,1,512,128]{3,2,1,0:T(8,128)(2,1)}), bf16[64,1,512,128]{3,2,1,0:T(8,128)(2,1)}, u32[]{:S(2)}, u32[]{:S(2)}) async-start(bf16[64,1,512,128]{3,2,1,0:T(8,128)(2,1)} %bitcast.80), calls=%async_computation | async-start | bytes 16777216 | tf_op jit(solution)/shard_map/all_to_all | solution.py:25
  35.3 258.9 %reduce-scatter.5.cloned.1.call-start = ((), (), s32[]{:S(2)}) async-start(), calls=%async_computation.6 | async-start | bytes 7864320 | tf_op jit(solution)/shard_map/reduce_scatter | solution.py:44
  221.1 4.5 copy-start.2
  230.8 104.8 %reduce-scatter.7.cloned.1.call-start = ((), (), s32[]{:S(2)}) async-start(), calls=%async_computation.7 | async-start | bytes 2621440 | tf_op jit(solution)/shard_map/reduce_scatter | solution.py:51
  298.9 6.4 %copy-start.8 = (s32[2,2]{1,0:T(2,128)S(1)}, s32[2,2]{1,0:T(2,128)}, u32[]{:S(2)}) copy-start(s32[2,2]{1,0:T(2,128)} %param.17) | copy-start | bytes 52
  299.0 8.5 %copy-start.9 = (s32[2]{0:T(128)S(1)}, s32[2]{0:T(128)}, u32[]{:S(2)}) copy-start(s32[2]{0:T(128)} %param.16) | copy-start | bytes 28
  300.9 19.0 %all-to-all-start.1 = ((bf16[2,3,128,512]{2,0,1,3:T(2,128)(2,1)}), bf16[2,3,128,512]{2,0,1,3:T(2,128)(2,1)}, u32[]{:S(2)}, u32[]{:S(2)}) async-start(bf16[2,3,128,512]{2,0,1,3:T(2,128)(2,1)} %copy.218), calls=%async_computation.3 | async-start | bytes 1572864 | tf_op jit(solution)/shard_map/all_to_all | solution.py:71
  305.1 104.8 %reduce-scatter.9.cloned.1.call-start = ((), (), s32[]{:S(2)}) async-start(), calls=%async_computation.8 | async-start | bytes 7864320 | tf_op jit(solution)/shard_map/reduce_scatter | solution.py:44
  321.2 14.4 %copy-start.3 = (f32[2,128,512]{1,2,0:T(8,128)S(1)}, f32[2,128,512]{1,2,0:T(8,128)}, u32[]{:S(2)}) copy-start(f32[2,128,512]{1,2,0:T(8,128)} %copy.214) | copy-start | bytes 1572868
  321.6 15.7 %copy-start.4 = (bf16[4,2,512,128]{3,2,1,0:T(8,128)(2,1)S(1)}, bf16[4,2,512,128]{3,2,1,0:T(8,128)(2,1)}, u32[]{:S(2)}) copy-start(bf16[4,2,512,128]{3,2,1,0:T(8,128)(2,1)} %gather_fusion.10) | copy-start | bytes 3145732
  322.3 15.0 %copy-start.5 = (bf16[2,3,128,512]{3,2,1,0:T(8,128)(2,1)S(1)}, bf16[2,3,128,512]{3,2,1,0:T(8,128)(2,1)}, u32[]{:S(2)}) copy-start(bf16[2,3,128,512]{3,2,1,0:T(8,128)(2,1)} %param.14) | copy-start | bytes 2359300
  343.7 102.0 %reduce-scatter.11.cloned.1.call-start = ((), (), s32[]{:S(2)}) async-start(), calls=%async_computation.9 | async-start | bytes 2621440 | tf_op jit(solution)/shard_map/reduce_scatter | solution.py:51
  409.9 3.6 copy-start.7
  413.5 34.3 %copy-start.1 = (s32[128]{0:T(128)S(1)}, s32[128]{0:T(128)}, u32[]{:S(2)}) copy-start(s32[128]{0:T(128)} %param.10) | copy-start | bytes 1540
Sparse Core Ops, SparseCore 0:
  230.9 63.2 reduce-scatter.4
  299.1 36.3 reduce-scatter.6
  343.8 66.0 reduce-scatter.8
  413.6 31.9 reduce-scatter.10
where the time goes:
time: 455 us; the launch traced here: 454 us
  waiting for transfers between devices  361 us (79%)
  local copies, waits for them, and re-layouts  44.4 us (10%)
  starting transfers between devices  17.7 us (4%)
  between operations  14.1 us (3%)
  matrix products  11.6 us (3%)
  other arithmetic  5.14 us (1%)
    all_to_all x1, waiting for transfers between devices, fetch_tiles(): lax.all_to_all(outgoing, 'own', split_axis=0, concat_axis=0, tiled=True)  186 us
    reduce_scatter x2, waiting for transfers between devices, solve_level(): lax.psum_scatter(product.reshape(groups * unit_rows, width), 'col', scatt...  130 us
    reduce_scatter x2, waiting for transfers between devices, solve_level(): lax.psum_scatter(partial_diag, 'col', scatter_dimension=1, tiled=True)  42.7 us
    all_to_all x1, starting transfers between devices, fetch_tiles(): lax.all_to_all(outgoing, 'own', split_axis=0, concat_axis=0, tiled=True)  13.2 us
  transfers between devices with their start and end apart: 6, of which 6 were waited for; matrix products, arithmetic and copies ran while one was open for 4% of the time, Pallas kernels for 0%

commit v1 on v0

v1 whole, which is shorter than its diff:
```python
import jax
import jax.numpy as jnp
from jax import lax
from jax.sharding import PartitionSpec as P


def assemble(low, cols, diag_cols, tiles, choose):
    top = jnp.concatenate([diag_cols.T[None], jnp.swapaxes(cols[choose], 1, 2)], 0)
    lower = jnp.concatenate([low[choose][:, None], tiles[choose][:, choose]], 1)
    return jnp.concatenate([top[None], lower], 0)


def solve_cross(tiles, factor):
    return -jnp.einsum("mikrs,mksj->mirj", tiles, factor, preferred_element_type=jnp.float32)


def correction(factor, cols):
    return jnp.einsum("mksj,mksl->mjl", factor, cols, preferred_element_type=jnp.float32)


def to_columns(rows):
    last = rows.ndim - 1
    return lax.all_to_all(rows, "col", split_axis=last, concat_axis=last - 1, tiled=True)


def to_rows(columns):
    last = columns.ndim - 1
    return lax.all_to_all(columns, "col", split_axis=last - 1, concat_axis=last, tiled=True)


def per_device(anc_store, block_map, anc_refs, factor1, dinv1, factor2, dinv2, parent, picked):
    blocks_here = factor1.shape[0]
    me = lax.axis_index("own")
    rows = to_rows(anc_store.astype(jnp.bfloat16))
    store = lax.all_gather(rows, "own", axis=0, tiled=True)
    whole1 = lax.all_gather(factor1, "col", axis=2, tiled=True)
    whole2 = lax.all_gather(factor2, "col", axis=2, tiled=True)
    dinv_cols1 = to_columns(dinv1)
    refs = lax.dynamic_slice_in_dim(anc_refs, me * blocks_here, blocks_here, 0)
    tiles1 = store[block_map[refs]]
    cross1 = solve_cross(tiles1, whole1)
    low1 = cross1.astype(jnp.bfloat16)
    cols1 = to_columns(low1)
    diag_cols1 = dinv_cols1 - correction(whole1, cols1)
    diag1 = to_rows(diag_cols1)
    tiles2 = jax.vmap(assemble)(
        low1[parent], cols1[parent], diag_cols1.astype(jnp.bfloat16)[parent], tiles1[parent], picked
    )
    cross2 = solve_cross(tiles2, whole2)
    cols2 = to_columns(cross2.astype(jnp.bfloat16))
    diag2 = dinv2 - to_rows(correction(whole2, cols2))
    return (cross1, diag1, cross2, diag2)


def solution(mesh):
    return jax.shard_map(
        per_device,
        mesh=mesh,
        in_specs=(
            P("own", None, "col"),
            P(),
            P(),
            P("own", None, "col", None),
            P("own", "col", None),
            P("own", None, "col", None),
            P("own", "col", None),
            P("own"),
            P("own", None),
        ),
        out_specs=(
            P("own", None, "col", None),
            P("own", "col", None),
            P("own", None, "col", None),
            P("own", "col", None),
        ),
        check_vma=False,
    )
```

time: 455 us -> 266 us (0.58)
  waiting for transfers between devices: 361 us -> 169 us
  blocking collectives: 0 us -> 10.4 us
  local copies, waits for them, and re-layouts: 44.4 us -> 36.2 us
    reduce_scatter x4 -> x0, waiting for transfers between devices: 172 us -> none  [the longest x2 130 us: solve_level(): lax.psum_scatter(product.reshape(groups * unit_rows, width), 'col', scatt...]
    all_to_all x2 -> x5, waiting for transfers between devices: 189 us -> 19.8 us  [the longest x3 10.9 us: to_columns(): lax.all_to_all(rows, 'col', split_axis=last, concat_axis=last - 1, tiled=...]
    all_gather x0 -> x3, waiting for transfers between devices: none -> 148 us  [the longest x1 94.7 us: per_device(): store = lax.all_gather(rows, 'own', axis=0, tiled=True)]
    all_to_all x0 -> x1, blocking collectives: none -> 10.4 us  [to_rows(): lax.all_to_all(columns, 'col', split_axis=last - 1, concat_axis=last, til...]
    gather x16 -> x12, local copies, waits for them, and re-layouts: 26.7 us -> 16.3 us  [the longest x3 7.25 us: per_device(): tiles1 = store[block_map[refs]]]
    all_to_all x2 -> x13, local copies, waits for them, and re-layouts: 1.65 us -> 9 us  [the longest x6 6.03 us: to_columns(): lax.all_to_all(rows, 'col', split_axis=last, concat_axis=last - 1, tiled=...]
    transpose x2 -> x0, local copies, waits for them, and re-layouts: 6.7 us -> none  [solve_level(): jnp.einsum('mikgrp,mkpj->gmirj', row_part, negated, preferred_element_typ...]
    all_to_all x2 -> x5, starting transfers between devices: 17.3 us -> 18.1 us  [the longest x3 11.1 us: to_columns(): lax.all_to_all(rows, 'col', split_axis=last, concat_axis=last - 1, tiled=...]
  transfers between devices with their start and end apart: 6 -> 8, of which waited for: 6 -> 6; matrix products, arithmetic and copies ran while one was open for 4% -> 14% of each run, Pallas kernels for 0% -> 0%
where the time goes in v1:
time: 266 us; the launch traced here: 263 us
  waiting for transfers between devices  169 us (64%)
  local copies, waits for them, and re-layouts  36.2 us (14%)
  starting transfers between devices  18.2 us (7%)
  matrix products  14.2 us (5%)
  between operations  14.1 us (5%)
  blocking collectives  10.4 us (4%)
    all_gather x1, waiting for transfers between devices, per_device(): store = lax.all_gather(rows, 'own', axis=0, tiled=True)  94.7 us
    all_gather x1, waiting for transfers between devices, per_device(): whole1 = lax.all_gather(factor1, 'col', axis=2, tiled=True)  34.1 us
    all_gather x1, waiting for transfers between devices, per_device(): whole2 = lax.all_gather(factor2, 'col', axis=2, tiled=True)  18.8 us
    all_to_all x3, starting transfers between devices, to_columns(): lax.all_to_all(rows, 'col', split_axis=last, concat_axis=last - 1, tiled=...  11.1 us
    all_to_all x3, waiting for transfers between devices, to_columns(): lax.all_to_all(rows, 'col', split_axis=last, concat_axis=last - 1, tiled=...  10.9 us
    all_to_all x1, blocking collectives, to_rows(): lax.all_to_all(columns, 'col', split_axis=last - 1, concat_axis=last, til...  10.4 us
    dot_general x2, matrix products, solve_cross(): jnp.einsum('mikrs,mksj->mirj', tiles, factor, preferred_element_type=jnp....  9.18 us
    all_to_all x2, waiting for transfers between devices, to_rows(): lax.all_to_all(columns, 'col', split_axis=last - 1, concat_axis=last, til...  8.95 us
  transfers between devices with their start and end apart: 8, of which 6 were waited for; matrix products, arithmetic and copies ran while one was open for 14% of the time, Pallas kernels for 0%

profile of v1, /device:TPU:1, one launch (start us, length us, event | category | flops | bytes accessed | tf_op | source)
XLA Modules:
  0.0 262.8 jit_solution(5023315494501467761)
XLA Ops:
  7.2 1.5 copy.111
  8.7 10.4 %all_to_all.108 = bf16[2,512,128]{2,0,1:T(2,128)(2,1)S(1)} all-to-all(bf16[2,512,128]{2,0,1:T(2,128)(2,1)S(1)} %copy.111), channel_id=1, replica_groups=mesh['own'=64,'col'=4] {'col'}, dimensions={1} | all-to-all | bytes 524288 | tf_op jit(solution)/shard_map/all_to_all | solution.py:28
  19.3 0.9 copy.85
  21.7 1.0 copy.87
  22.7 4.1 %all-to-all-start.1 = ((f32[2,128,512]{1,0,2:T(2,128)}), f32[2,128,512]{1,0,2:T(2,128)}, u32[]{:S(2)}, u32[]{:S(2)}) async-start(f32[2,128,512]{1,0,2:T(2,128)} %copy.87), calls=%async_computation.1 | async-start | bytes 1048576 | tf_op jit(solution)/shard_map/all_to_all | solution.py:23
  28.1 94.7 %all-gather.4.cloned.1.call-done = bf16[128,128,512]{2,1,0:T(8,128)(2,1)} async-done(((bf16[2,128,512]{2,1,0:T(8,128)(2,1)}), bf16[128,128,512]{2,1,0:T(8,128)(2,1)}) %all-gather.4.cloned.1.call-update) | async-done | bytes 16777232 | tf_op jit(solution)/shard_map/all_gather | solution.py:35
  122.8 6.5 %gather_fusion.1 = bf16[18,128,512]{2,1,0:T(8,128)(2,1)S(1)} fusion(bf16[128,128,512]{2,1,0:T(8,128)(2,1)} %all-gather.4.cloned.1.call-done, s32[1024]{0:T(1024)S(1)} %pad_clamp_fusion.1), kind=kCustom, calls=%fused_computation.1 | custom fusion | bytes 4718664 | tf_op jit(solution)/shard_map/gather | solution.py:40
  129.3 34.1 %all-gather.6.cloned.1.call-done = bf16[2,3,512,512]{3,2,1,0:T(8,128)(2,1)} async-done(((bf16[2,3,128,512]{3,2,1,0:T(8,128)(2,1)}), bf16[2,3,512,512]{3,2,1,0:T(8,128)(2,1)}) %all-gather.6.cloned.1.call-update) | async-done | bytes 3145744 | tf_op jit(solution)/shard_map/all_gather | solution.py:36
  163.4 4.4 %fusion.21 = (bf16[2,3,128,512]{3,2,1,0:T(8,128)(2,1)S(1)}, f32[2,3,128,512]{3,2,1,0:T(8,128)}) fusion(bf16[2,3,3,128,512]{4,3,2,1,0:T(8,128)(2,1)S(1)} %bitcast.96, bf16[2,3,512,512]{3,2,1,0:T(8,128)(2,1)} %all-gather.6.cloned.1.call-done), kind=kOutput, calls=%fused_computation.42 | convolution fusion | flops 1208745984 | bytes 7864320 | tf_op jit(solution)/shard_map/mikrs,mksj->mirj/dot_general | solution.py:14
  167.8 1.8 copy.89
  169.6 3.5 %all-to-all-start.2 = ((bf16[2,3,128,512]{2,0,1,3:T(2,128)(2,1)}), bf16[2,3,128,512]{2,0,1,3:T(2,128)(2,1)S(1)}, u32[]{:S(2)}, u32[]{:S(2)}) async-start(bf16[2,3,128,512]{2,0,1,3:T(2,128)(2,1)} %copy.89), calls=%async_computation.2 | async-start | bytes 1572864 | tf_op jit(solution)/shard_map/all_to_all | solution.py:23
  173.2 2.2 copy.115
  175.4 2.0 all_to_all.85
  177.5 2.1 gather_fusion.5
  179.6 2.7 %gather_fusion.4 = bf16[2,3,128,512]{3,2,1,0:T(8,128)(2,1)} fusion(bf16[2,3,128,512]{3,2,1,0:T(8,128)(2,1)} %copy-done.1, s32[1024]{0:T(1024)S(1)} %pad_clamp_fusion), kind=kCustom, calls=%fused_computation.4 | custom fusion | bytes 1572872 | tf_op jit(solution)/shard_map/gather | solution.py:47
  182.2 2.3 gather_fusion.8
  185.2 1.1 copy.112
  189.3 2.5 fusion.22
  192.5 18.8 %all-gather.8.cloned.1.call-done = bf16[2,3,512,512]{3,2,1,0:T(8,128)(2,1)} async-done(((bf16[2,3,128,512]{3,2,1,0:T(8,128)(2,1)}), bf16[2,3,512,512]{3,2,1,0:T(8,128)(2,1)}) %all-gather.8.cloned.1.call-update) | async-done | bytes 3145744 | tf_op jit(solution)/shard_map/all_gather | solution.py:37
  211.2 4.8 %fusion.23 = (bf16[2,3,128,512]{3,2,1,0:T(8,128)(2,1)S(1)}, f32[2,3,128,512]{3,2,1,0:T(8,128)}) fusion(bf16[2,3,512,512]{3,2,1,0:T(8,128)(2,1)} %all-gather.8.cloned.1.call-done, bf16[2,2,2,128,512]{4,3,2,1,0:T(8,128)(2,1)} %bitcast.108, bf16[2,2,1,128,512]{4,3,2,1,0:T(8,128)(2,1)S(1)} %bitcast.112, bf16[2,1,3,128,512]{4,3,2,1,0:T(8,128)(2,1)S(1)} %maximum_bitcast_fusion), kind=kOutput, calls=%fused_computation.44 | convolution fusion | flops 1211105280 | bytes 7864320 | tf_op jit(solution)/shard_map/mikrs,mksj->mirj/dot_general | solution.py:14
  216.0 1.9 copy.96
  217.8 3.5 %all-to-all-start.4 = ((bf16[2,3,128,512]{2,0,1,3:T(2,128)(2,1)}), bf16[2,3,128,512]{2,0,1,3:T(2,128)(2,1)S(1)}, u32[]{:S(2)}, u32[]{:S(2)}) async-start(bf16[2,3,128,512]{2,0,1,3:T(2,128)(2,1)} %copy.96), calls=%async_computation.4 | async-start | bytes 1572864 | tf_op jit(solution)/shard_map/all_to_all | solution.py:23
  221.3 1.0 copy.91
  222.3 10.9 %all-to-all-done.4 = bf16[2,3,128,512]{2,0,1,3:T(2,128)(2,1)S(1)} async-done(((bf16[2,3,128,512]{2,0,1,3:T(2,128)(2,1)}), bf16[2,3,128,512]{2,0,1,3:T(2,128)(2,1)S(1)}, u32[]{:S(2)}, u32[]{:S(2)}) %all-to-all-start.4) | async-done | bytes 786464 | tf_op jit(solution)/shard_map/all_to_all | solution.py:23
  233.2 3.5 %all-to-all-start.3 = ((f32[2,512,128]{2,0,1:T(2,128)}), f32[2,512,128]{2,0,1:T(2,128)S(1)}, u32[]{:S(2)}, u32[]{:S(2)}) async-start(f32[2,512,128]{2,0,1:T(2,128)} %copy.91), calls=%async_computation.3 | async-start | bytes 1048576 | tf_op jit(solution)/shard_map/all_to_all | solution.py:28
  237.6 2.5 convolution_bitcast_fusion
  240.1 1.0 copy.98
  241.1 3.4 %all-to-all-done.3 = f32[2,512,128]{2,0,1:T(2,128)S(1)} async-done(((f32[2,512,128]{2,0,1:T(2,128)}), f32[2,512,128]{2,0,1:T(2,128)S(1)}, u32[]{:S(2)}, u32[]{:S(2)}) %all-to-all-start.3) | async-done | bytes 524320 | tf_op jit(solution)/shard_map/all_to_all | solution.py:28
  244.5 3.5 %all-to-all-start.5 = ((f32[2,512,128]{2,0,1:T(2,128)}), f32[2,512,128]{2,0,1:T(2,128)S(1)}, u32[]{:S(2)}, u32[]{:S(2)}) async-start(f32[2,512,128]{2,0,1:T(2,128)} %copy.98), calls=%async_computation.5 | async-start | bytes 1048576 | tf_op jit(solution)/shard_map/all_to_all | solution.py:28
  248.3 1.0 all_to_all.93
  249.3 5.5 %all-to-all-done.5 = f32[2,512,128]{2,0,1:T(2,128)S(1)} async-done(((f32[2,512,128]{2,0,1:T(2,128)}), f32[2,512,128]{2,0,1:T(2,128)S(1)}, u32[]{:S(2)}, u32[]{:S(2)}) %all-to-all-start.5) | async-done | bytes 524320 | tf_op jit(solution)/shard_map/all_to_all | solution.py:28
  255.4 0.9 sub.7
  (54 shorter events, 9.0 us)
Async XLA Ops:
  7.2 20.0 %copy-start = (s32[128]{0:T(128)S(1)}, s32[128]{0:T(128)}, u32[]{:S(2)}) copy-start(s32[128]{0:T(128)} %param.10) | copy-start | bytes 1540
  7.2 14.5 %copy-start.5 = (f32[2,128,512]{2,1,0:T(8,128)S(1)}, f32[2,128,512]{2,1,0:T(8,128)}, u32[]{:S(2)}) copy-start(f32[2,128,512]{2,1,0:T(8,128)} %param.13) | copy-start | bytes 1572868
  7.2 115.6 %all-gather.4.cloned.1.call-start = ((), (), s32[]{:S(2)}) async-start(), calls=%async_computation.6 | async-start | bytes 17039360 | tf_op jit(solution)/shard_map/all_gather | solution.py:35
  19.3 7.5 %copy-start.6 = (s32[128,3,3]{0,2,1:T(4,128)S(1)}, s32[128,3,3]{0,2,1:T(4,128)}, u32[]{:S(2)}) copy-start(s32[128,3,3]{0,2,1:T(4,128)} %param.11) | copy-start | bytes 13828
  20.2 143.1 %all-gather.6.cloned.1.call-start = ((), (), s32[]{:S(2)}) async-start(), calls=%async_computation.7 | async-start | bytes 3932160 | tf_op jit(solution)/shard_map/all_gather | solution.py:36
  21.0 190.2 %all-gather.8.cloned.1.call-start = ((), (), s32[]{:S(2)}) async-start(), calls=%async_computation.8 | async-start | bytes 3932160 | tf_op jit(solution)/shard_map/all_gather | solution.py:37
  22.7 146.9 %all-to-all-start.1 = ((f32[2,128,512]{1,0,2:T(2,128)}), f32[2,128,512]{1,0,2:T(2,128)}, u32[]{:S(2)}, u32[]{:S(2)}) async-start(f32[2,128,512]{1,0,2:T(2,128)} %copy.87), calls=%async_computation.1 | async-start | bytes 1048576 | tf_op jit(solution)/shard_map/all_to_all | solution.py:23
  167.8 1.8 copy-start.1
  167.8 5.3 %copy-start.7 = (s32[2,2]{1,0:T(2,128)S(1)}, s32[2,2]{1,0:T(2,128)}, u32[]{:S(2)}) copy-start(s32[2,2]{1,0:T(2,128)} %param.17) | copy-start | bytes 52
  167.8 5.4 %copy-start.8 = (s32[2]{0:T(128)S(1)}, s32[2]{0:T(128)}, u32[]{:S(2)}) copy-start(s32[2]{0:T(128)} %param.16) | copy-start | bytes 28
  169.6 17.5 %all-to-all-start.2 = ((bf16[2,3,128,512]{2,0,1,3:T(2,128)(2,1)}), bf16[2,3,128,512]{2,0,1,3:T(2,128)(2,1)S(1)}, u32[]{:S(2)}, u32[]{:S(2)}) async-start(bf16[2,3,128,512]{2,0,1,3:T(2,128)(2,1)} %copy.89), calls=%async_computation.2 | async-start | bytes 1572864 | tf_op jit(solution)/shard_map/all_to_all | solution.py:23
  185.2 1.4 copy-start.2
  187.8 1.5 copy-start.3
  217.8 15.4 %all-to-all-start.4 = ((bf16[2,3,128,512]{2,0,1,3:T(2,128)(2,1)}), bf16[2,3,128,512]{2,0,1,3:T(2,128)(2,1)S(1)}, u32[]{:S(2)}, u32[]{:S(2)}) async-start(bf16[2,3,128,512]{2,0,1,3:T(2,128)(2,1)} %copy.96), calls=%async_computation.4 | async-start | bytes 1572864 | tf_op jit(solution)/shard_map/all_to_all | solution.py:23
  233.2 11.3 %all-to-all-start.3 = ((f32[2,512,128]{2,0,1:T(2,128)}), f32[2,512,128]{2,0,1:T(2,128)S(1)}, u32[]{:S(2)}, u32[]{:S(2)}) async-start(f32[2,512,128]{2,0,1:T(2,128)} %copy.91), calls=%async_computation.3 | async-start | bytes 1048576 | tf_op jit(solution)/shard_map/all_to_all | solution.py:28
  244.5 10.4 %all-to-all-start.5 = ((f32[2,512,128]{2,0,1:T(2,128)}), f32[2,512,128]{2,0,1:T(2,128)S(1)}, u32[]{:S(2)}, u32[]{:S(2)}) async-start(f32[2,512,128]{2,0,1:T(2,128)} %copy.98), calls=%async_computation.5 | async-start | bytes 1048576 | tf_op jit(solution)/shard_map/all_to_all | solution.py:28
  248.0 7.5 %copy-start.4 = (f32[2,128,512]{2,1,0:T(8,128)S(1)}, f32[2,128,512]{2,1,0:T(8,128)}, u32[]{:S(2)}) copy-start(f32[2,128,512]{2,1,0:T(8,128)} %param.15) | copy-start | bytes 1572868
Sparse Core Ops, SparseCore 0:
  20.3 102.4 all-gather.3
  124.6 38.6 all-gather.5
  165.2 46.0 all-gather.7

commit v2 on v1

v2 whole, which is shorter than its diff:
```python
import functools

import jax
import jax.numpy as jnp
from jax import lax
from jax.experimental import pallas as pl
from jax.experimental.pallas import tpu as pltpu
from jax.sharding import PartitionSpec as P

X, Z, Y = 4, 8, 4
B, A, W = 512, 3, 128
ROWS_A = 48
F32, BF16 = jnp.float32, jnp.bfloat16


class Wires:
    def __init__(self, send_sems, recv_sems):
        self.send_sems, self.recv_sems = send_sems, recv_sems
        self.names, self.sent = {}, []

    def slot(self, name):
        return self.names.setdefault(name, len(self.names))

    def make(self, name, src, dst, device):
        slot = self.slot(name)
        return pltpu.make_async_remote_copy(
            src_ref=src,
            dst_ref=dst,
            send_sem=self.send_sems.at[slot],
            recv_sem=self.recv_sems.at[slot],
            device_id=device,
            device_id_type=pl.DeviceIdType.MESH,
        )

    def send(self, name, src, dst, device):
        copy = self.make(name, src, dst, device)
        copy.start()
        self.sent.append(copy)

    def wait(self, name, dst, device):
        self.make(name, dst, dst, device).wait_recv()

    def finish(self):
        for copy in self.sent:
            copy.wait_send()


WIRES = 256


def dot(a, b):
    return jnp.dot(a, b, preferred_element_type=F32)


def kernel(
    anc, bmap, refs_all, f1, dinv1, f2, dinv2, parent, picked,
    cross1, diag1, cross2, diag2,
    store, f1w, f2w, anc_v, stage, refs, low, turned, turned2, cols1, cols2, out1, out2,
    part, dcol, dcolt, dlow, dsend1, dsend2, grow, dinv_v, dout,
    send_sems, recv_sems, local_sems,
):
    own, y = lax.axis_index("own"), lax.axis_index("col")
    core = lax.rem(own, 2)
    chip = own // 2
    x, z = chip // Z, lax.rem(chip, Z)

    def at(dx, dz, dcore=0):
        xx, zz = lax.rem(x + dx + X, X), lax.rem(z + dz + Z, Z)
        return (xx * Z + zz) * 2 + (lax.rem(core + dcore, 2) if dcore else core)

    def yat(d):
        return lax.rem(y + d + Y, Y)

    xup, xdn = (at(1, 0), y), (at(-1, 0), y)
    zup, zdn = (at(0, 1), y), (at(0, -1), y)
    mate = (at(0, 0, 1), y)
    ydev = {d: (own, yat(d)) for d in (1, 2, 3)}
    wires = Wires(send_sems, recv_sems)
    held = {}

    def local(name, src, dst):
        slot = held.setdefault(name, len(held))
        return pltpu.make_async_copy(src, dst, local_sems.at[slot])

    def lanes(index):
        return pl.ds(pl.multiple_of(index * W, W), W)

    load_anc = local("anc", anc, anc_v)
    load_anc.start()
    load_refs = local("refs", refs_all.at[pl.ds(own * 2, 2)], refs)
    load_refs.start()
    load_f1 = local("f1", f1, f1w.at[:, :, lanes(y), :])
    load_f1.start()
    load_f2 = local("f2", f2, f2w.at[:, :, lanes(y), :])
    load_f2.start()
    load_dcol = local("dcol", dinv1.at[:, :, lanes(y)], dcol.at[:, lanes(y), :])
    load_dcol.start()
    load_dinv2 = local("dinv2", dinv2, dinv_v)
    load_dinv2.start()

    barrier = pltpu.get_barrier_semaphore()
    peers = [xup, xdn, zup, zdn, mate, ydev[1], ydev[2], ydev[3]]
    for peer in peers:
        pl.semaphore_signal(barrier, inc=1, device_id=peer, device_id_type=pl.DeviceIdType.MESH)
    pl.semaphore_wait(barrier, len(peers))

    load_anc.wait()
    stage[...] = anc_v[...].astype(BF16)
    mine = pl.ds(own * 2, 2)
    for d in (1, 3, 2):
        wires.send(("t", d), stage.at[:, lanes(yat(d)), :], store.at[mine, :, lanes(y)], ydev[d])
    keep = local("t", stage.at[:, lanes(y), :], store.at[mine, :, lanes(y)])
    keep.start()

    def factor_own(tag, src, dst):
        for m, k in ((0, 1), (1, 0)):
            wires.send((tag, "up", m), src.at[m], dst.at[m, :, lanes(y), :], ydev[1])
            wires.send((tag, "dn", k), src.at[k], dst.at[k, :, lanes(y), :], ydev[3])

    def factor_wait(tag, dst, first):
        for way, d, m in (("up", -1, 0 if first else 1), ("dn", 1, 1 if first else 0)):
            piece = dst.at[m, :, lanes(yat(d)), :]
            wires.wait((tag, way, m), piece, ydev[3 if d == -1 else 1])
            if first:
                wires.send((tag, way, "far"), piece, piece, ydev[1 if d == -1 else 3])

    def factor_far(tag, dst):
        wires.wait((tag, "up", "far"), dst.at[0, :, lanes(yat(2)), :], ydev[3])
        wires.wait((tag, "dn", "far"), dst.at[1, :, lanes(yat(2)), :], ydev[1])

    factor_own("f1", f1, f1w)

    keep.wait()
    for d in (1, 3, 2):
        wires.wait(("t", d), store.at[mine, :, lanes(yat(-d))], ydev[4 - d])

    def chunk(path, dx, dz, slot=None, dcore=0):
        tile = at(dx, dz, dcore) * 2
        tiles = pl.ds(tile, 2) if slot is None else pl.ds(tile + slot, 1)
        rows = pl.ds(0, ROWS_A) if path == "a" else pl.ds(ROWS_A, W - ROWS_A)
        return store.at[tiles, rows, :]

    def share(path, dx, dz, slot=None):
        piece = chunk(path, dx, dz, slot)
        wires.send(("mate", path, dx, dz, slot), piece, piece, mate)
        shared.append((path, dx, dz, slot))

    shared = []
    ZWAY = {"up": (zup, zdn, -1), "dn": (zdn, zup, 1)}
    XWAY = {"up": (xup, xdn, -1), "dn": (xdn, xup, 1)}
    SLOT = {"up": 0, "dn": 1}

    def z_send(path, dx, step, slot=None):
        for way, (to, _, sign) in ZWAY.items():
            half = SLOT[way] if step == 4 else slot
            piece = chunk(path, dx, sign * (step - 1), half)
            wires.send(("z", path, dx, way, step), piece, piece, to)

    def x_send(path, dz):
        piece = chunk(path, 0, dz)
        for way, (to, _, _) in XWAY.items():
            wires.send(("x", path, dz, way, 1), piece, piece, to)

    def z_wait(path, dx, step):
        for way, (to, source, sign) in ZWAY.items():
            half = SLOT[way] if step == 4 else None
            piece = chunk(path, dx, sign * step, half)
            wires.wait(("z", path, dx, way, step), piece, source)
            if step < 4:
                half = SLOT[way] if step == 3 else None
                on = chunk(path, dx, sign * step, half)
                wires.send(("z", path, dx, way, step + 1), on, on, to)
                if path == "b":
                    x_send("b", sign * step)
                share(path, dx, sign * step)
        if step == 4:
            if path == "b":
                x_send("b", 4)
            share(path, dx, 4)

    def x_wait(path, dz):
        for way, (to, source, sign) in XWAY.items():
            piece = chunk(path, sign, dz)
            wires.wait(("x", path, dz, way, 1), piece, source)
            on = chunk(path, sign, dz, SLOT[way])
            wires.send(("x", path, dz, way, 2), on, on, to)
            if path == "a":
                z_send("a", sign, 1)
            share(path, sign, dz)

    def x_far(path, dz):
        for way, (_, source, _) in XWAY.items():
            wires.wait(("x", path, dz, way, 2), chunk(path, 2, dz, SLOT[way]), source)
        if path == "a":
            z_send("a", 2, 1)
        share(path, 2, dz)

    x_send("a", 0)
    z_send("b", 0, 1)
    z_send("a", 0, 1)
    x_send("b", 0)
    share("a", 0, 0)
    share("b", 0, 0)

    x_wait("a", 0)
    z_wait("b", 0, 1)
    x_wait("b", 0)
    z_wait("a", 0, 1)
    x_far("a", 0)
    z_wait("b", 0, 2)
    x_far("b", 0)
    factor_wait("f1", f1w, True)
    x_wait("b", -1)
    z_wait("a", -1, 1)
    x_wait("b", 1)
    z_wait("a", 1, 1)
    x_far("b", -1)
    z_wait("b", 0, 3)
    x_far("b", 1)
    factor_wait("f1", f1w, False)
    factor_own("f2", f2, f2w)
    for d in (1, 3, 2):
        wires.send(("d", d), dinv1.at[:, :, lanes(yat(d))], dcol.at[:, lanes(y), :], ydev[d])
    z_wait("a", 2, 1)
    x_wait("b", -2)
    z_wait("a", 0, 2)
    x_wait("b", 2)
    z_wait("b", 0, 4)
    x_far("b", -2)
    x_far("b", 2)
    z_wait("a", -1, 2)
    factor_far("f1", f1w)
    x_wait("b", -3)
    z_wait("a", 1, 2)
    x_wait("b", 3)
    z_wait("a", 2, 2)
    x_far("b", -3)
    x_far("b", 3)
    factor_wait("f2", f2w, True)
    z_wait("a", 0, 3)
    x_wait("b", 4)
    z_wait("a", -1, 3)
    x_far("b", 4)
    z_wait("a", 1, 3)
    z_wait("a", 2, 3)
    for dx in (0, -1, 1, 2):
        z_wait("a", dx, 4)
    for path, dx, dz, slot in shared:
        wires.wait(("mate", path, dx, dz, slot), chunk(path, dx, dz, slot, 1), mate)
    load_refs.wait()
    load_f1.wait()

    def tile(m, i, k):
        return store[bmap[refs[m, i, k]]]

    def stacked(parts):
        return jnp.concatenate(parts, axis=0)

    def give_columns(tag, turned_ref, cols_ref, m):
        for d in (1, 3, 2):
            wires.send(
                (tag, m, d), turned_ref.at[yat(d), m], cols_ref.at[m, :, :, lanes(y)], ydev[d]
            )
        own_part = local((tag, m), turned_ref.at[y, m], cols_ref.at[m, :, :, lanes(y)])
        own_part.start()
        return own_part

    def take_columns(tag, cols_ref, m, own_part):
        own_part.wait()
        for d in (1, 3, 2):
            wires.wait((tag, m, d), cols_ref.at[m, :, :, lanes(yat(-d))], ydev[4 - d])

    def spread(acc, m, n, out_ref, turned_ref, low_ref):
        for i in range(A):
            rows = acc[i * W : (i + 1) * W]
            out_ref[m, i, :, n * 256 : (n + 1) * 256] = rows
            if low_ref is not None:
                low_ref[m, i, :, n * 256 : (n + 1) * 256] = rows.astype(BF16)
            for b in range(2):
                turned_ref[2 * n + b, m, i] = rows[:, b * W : (b + 1) * W].T.astype(BF16)

    kept1, writes = [], []
    for m in range(2):
        for n in range(2):
            acc = 0.0
            for k in range(A):
                acc += dot(
                    stacked([tile(m, i, k) for i in range(A)]), f1w[m, k, :, n * 256 : (n + 1) * 256]
                )
            spread(-acc, m, n, out1, turned, low)
        kept1.append(give_columns("c1", turned, cols1, m))
        write = local(("o1", m), out1.at[m], cross1.at[m])
        write.start()
        writes.append(write)

    factor_wait("f2", f2w, False)
    factor_far("f2", f2w)
    load_f2.wait()
    for m in range(2):
        p = parent[m]
        q = [picked[m, 0], picked[m, 1]]
        for n in range(2):
            acc = 0.0
            for k in range(2):
                acc += dot(
                    stacked([tile(p, q[i], q[k]) for i in range(2)]),
                    f2w[m, k + 1, :, n * 256 : (n + 1) * 256],
                )
            part[m, :, n * 256 : (n + 1) * 256] = acc
    load_dcol.wait()
    for d in (1, 3, 2):
        wires.wait(("d", d), dcol.at[:, lanes(yat(-d)), :], ydev[4 - d])
    for m in range(2):
        for b in range(Y):
            dcolt[m, :, b * W : (b + 1) * W] = dcol[m, b * W : (b + 1) * W, :].T

    def corrections(cols_ref, fw, m):
        return sum(dot(cols_ref[m, k], fw[m, k]) for k in range(A))

    for m in range(2):
        take_columns("c1", cols1, m, kept1[m])
        turned_diag = dcolt[m] - corrections(cols1, f1w, m)
        dlow[m] = turned_diag.astype(BF16)
        for b in range(Y):
            dsend1[b, m] = turned_diag[:, b * W : (b + 1) * W].T

    def give_rows(tag, src, dst):
        for d in (1, 3, 2):
            wires.send((tag, d), src.at[yat(d)], dst.at[:, :, lanes(y)], ydev[d])
        own_part = local(tag, src.at[y], dst.at[:, :, lanes(y)])
        own_part.start()
        return own_part

    def take_rows(tag, dst, own_part):
        own_part.wait()
        for d in (1, 3, 2):
            wires.wait((tag, d), dst.at[:, :, lanes(yat(-d))], ydev[4 - d])

    kept2 = []
    for m in range(2):
        p = parent[m]
        q = [picked[m, 0], picked[m, 1]]
        for n in range(2):
            span = slice(n * 256, (n + 1) * 256)
            acc = dot(stacked([dlow[p], low[p, q[0]], low[p, q[1]]]), f2w[m, 0, :, span])
            top = dot(cols1[p, q[0]], f2w[m, 1, :, span]) + dot(cols1[p, q[1]], f2w[m, 2, :, span])
            acc += stacked([top, part[m, :, span]])
            spread(-acc, m, n, out2, turned2, None)
        kept2.append(give_columns("c2", turned2, cols2, m))
        write = local(("o2", m), out2.at[m], cross2.at[m])
        write.start()
        writes.append(write)
    kept_diag = give_rows("g1", dsend1, diag1)
    load_dinv2.wait()
    for m in range(2):
        take_columns("c2", cols2, m, kept2[m])
        correction = corrections(cols2, f2w, m)
        for b in range(Y):
            dsend2[b, m] = correction[:, b * W : (b + 1) * W].T
    kept_grow = give_rows("g2", dsend2, grow)
    take_rows("g1", diag1, kept_diag)
    take_rows("g2", grow, kept_grow)
    dout[...] = dinv_v[...] - grow[...]
    write = local("o3", dout, diag2)
    write.start()
    writes.append(write)
    for write in writes:
        write.wait()
    wires.finish()


def per_device(anc_store, block_map, anc_refs, factor1, dinv1, factor2, dinv2, parent, picked):
    any_space = pl.BlockSpec(memory_space=pl.ANY)
    smem = pl.BlockSpec(memory_space=pltpu.SMEM)
    flops = 2 * 2 * 2 * (9 + 3) * W * B * B
    return pl.pallas_call(
        kernel,
        out_shape=(
            jax.ShapeDtypeStruct((2, A, W, B), F32),
            jax.ShapeDtypeStruct((2, W, B), F32),
            jax.ShapeDtypeStruct((2, A, W, B), F32),
            jax.ShapeDtypeStruct((2, W, B), F32),
        ),
        in_specs=[any_space, smem, any_space, any_space, any_space, any_space, any_space, smem, smem],
        out_specs=(any_space,) * 4,
        scratch_shapes=[
            pltpu.VMEM((X * Z * 4, W, B), BF16),
            pltpu.VMEM((2, A, B, B), BF16),
            pltpu.VMEM((2, A, B, B), BF16),
            pltpu.VMEM((2, B, W), F32),
            pltpu.VMEM((2, B, W), BF16),
            pltpu.SMEM((2, A, A), jnp.int32),
            pltpu.VMEM((2, A, W, B), BF16),
            pltpu.VMEM((Y, 2, A, W, W), BF16),
            pltpu.VMEM((Y, 2, A, W, W), BF16),
            pltpu.VMEM((2, A, W, B), BF16),
            pltpu.VMEM((2, A, W, B), BF16),
            pltpu.VMEM((2, A, W, B), F32),
            pltpu.VMEM((2, A, W, B), F32),
            pltpu.VMEM((2, 2 * W, B), F32),
            pltpu.VMEM((2, B, W), F32),
            pltpu.VMEM((2, W, B), F32),
            pltpu.VMEM((2, W, B), BF16),
            pltpu.VMEM((Y, 2, W, W), F32),
            pltpu.VMEM((Y, 2, W, W), F32),
            pltpu.VMEM((2, W, B), F32),
            pltpu.VMEM((2, W, B), F32),
            pltpu.VMEM((2, W, B), F32),
            pltpu.SemaphoreType.DMA((WIRES,)),
            pltpu.SemaphoreType.DMA((WIRES,)),
            pltpu.SemaphoreType.DMA((32,)),
        ],
        compiler_params=pltpu.CompilerParams(
            collective_id=0, has_side_effects=True, vmem_limit_bytes=56 * 1024 * 1024
        ),
        cost_estimate=pl.CostEstimate(flops=flops, bytes_accessed=8 << 20, transcendentals=0),
    )(anc_store, block_map, anc_refs, factor1, dinv1, factor2, dinv2, parent, picked)


def solution(mesh):
    return jax.shard_map(
        per_device,
        mesh=mesh,
        in_specs=(
            P("own", None, "col"),
            P(),
            P(),
            P("own", None, "col", None),
            P("own", "col", None),
            P("own", None, "col", None),
            P("own", "col", None),
            P("own"),
            P("own", None),
        ),
        out_specs=(
            P("own", None, "col", None),
            P("own", "col", None),
            P("own", None, "col", None),
            P("own", "col", None),
        ),
        check_vma=False,
    )
```

time: 266 us -> 120 us (0.45)
  waiting for transfers between devices: 169 us -> 0 us
  Pallas kernels: 0 us -> 111 us
  local copies, waits for them, and re-layouts: 36.2 us -> 7.44 us
  starting transfers between devices: 18.2 us -> 0 us
  matrix products: 14.2 us -> 0 us
  between operations: 14.1 us -> 0.66 us
  blocking collectives: 10.4 us -> 0 us
    all_gather x3 -> x0, waiting for transfers between devices: 148 us -> none  [the longest x1 94.7 us: per_device(): store = lax.all_gather(rows, 'own', axis=0, tiled=True)]
    pallas_call x0 -> x1, Pallas kernels: none -> 111 us  [per_device(): pl.pallas_call(kernel, out_shape=(jax.ShapeDtypeStruct((2, A, W, B), F32)...]
    all_to_all x5 -> x0, waiting for transfers between devices: 19.8 us -> none  [the longest x3 10.9 us: to_columns(): lax.all_to_all(rows, 'col', split_axis=last, concat_axis=last - 1, tiled=...]
    gather x13 -> x0, local copies, waits for them, and re-layouts: 18.5 us -> none  [the longest x3 7.25 us: per_device(): tiles1 = store[block_map[refs]]]
    all_to_all x5 -> x0, starting transfers between devices: 18.1 us -> none  [the longest x3 11.1 us: to_columns(): lax.all_to_all(rows, 'col', split_axis=last, concat_axis=last - 1, tiled=...]
    dot_general x4 -> x0, matrix products: 14.2 us -> none  [the longest x2 9.18 us: solve_cross(): jnp.einsum('mikrs,mksj->mirj', tiles, factor, preferred_element_type=jnp....]
    all_to_all x1 -> x0, blocking collectives: 10.4 us -> none  [to_rows(): lax.all_to_all(columns, 'col', split_axis=last - 1, concat_axis=last, til...]
    all_to_all x13 -> x0, local copies, waits for them, and re-layouts: 9 us -> none  [the longest x6 6.03 us: to_columns(): lax.all_to_all(rows, 'col', split_axis=last, concat_axis=last - 1, tiled=...]
  transfers between devices with their start and end apart: 8 -> 0, of which waited for: 6 -> 0; matrix products, arithmetic and copies ran while one was open for 14% -> 0% of each run, Pallas kernels for 0% -> 0%
where the time goes in v2:
time: 120 us; the launch traced here: 119 us
  Pallas kernels  111 us (92%)
  local copies, waits for them, and re-layouts  7.44 us (6%)
    pallas_call x1, Pallas kernels, per_device(): pl.pallas_call(kernel, out_shape=(jax.ShapeDtypeStruct((2, A, W, B), F32)...  111 us
    unnamed x11, local copies, waits for them, and re-layouts  7.44 us

profile of v2, /device:TPU:1, one launch (start us, length us, event | category | flops | bytes accessed | tf_op | source)
XLA Modules:
  0.0 119.4 jit_solution(11821081444312220245)
XLA Ops:
  0.6 1.5 %copy.13.refs_all = s32[128,3,3]{2,1,0:T(4,128)} copy(s32[128,3,3]{0,2,1:T(4,128)} %param.11) | data formatting | bytes 9216 | tf_op args[2]
  2.2 111.3 %shard_map.120 = (f32[2,3,128,512]{3,2,1,0:T(8,128)}, f32[2,128,512]{2,1,0:T(8,128)}, f32[2,3,128,512]{3,2,1,0:T(8,128)}, f32[2,128,512]{2,1,0:T(8,128)}) custom-call(f32[2,512,128]{2,1,0:T(8,128)} %anc.1, s32[128]{0:T(128)} %bmap.1, s32[128,3,3]{2,1,0:T(4,128)} %copy.13.refs_all, bf16[2,3,128,512]{3,2,1,0:T(8,128)(2,1)} %f1.1, f32[2,128,512]{2,1,0:T(8,128)} %dinv1.1, ...), custom_call_target="tpu_custom_call" | custom-call | flops 3221225472 | bytes 8388608 | tf_op jit(solution)/shard_map/pallas_call | solution.py:376
  113.5 0.0 copy-start.2
  113.5 0.0 copy-start
  113.5 2.9 %copy.18 = f32[2,3,128,512]{3,2,1,0:T(8,128)} copy(f32[2,3,128,512]{3,2,1,0:T(8,128)} %get-tuple-element.8) | data formatting | bytes 3145728
  116.4 0.0 copy-done.2
  116.4 0.8 copy.19
  117.2 0.0 copy-done
  117.2 0.0 copy-start.1
  117.2 1.1 copy.20
  118.3 0.3 copy-done.1
  118.6 0.8 copy.21
Async XLA Ops:
  113.5 2.9 %copy-start.2 = (f32[2,128,512]{2,1,0:T(8,128)S(1)}, f32[2,128,512]{2,1,0:T(8,128)}, u32[]{:S(2)}) copy-start(f32[2,128,512]{2,1,0:T(8,128)} %get-tuple-element.9) | copy-start | bytes 1572868
  113.5 3.7 %copy-start = (f32[2,3,128,512]{3,2,1,0:T(8,128)S(1)}, f32[2,3,128,512]{3,2,1,0:T(8,128)}, u32[]{:S(2)}) copy-start(f32[2,3,128,512]{3,2,1,0:T(8,128)} %get-tuple-element.10) | copy-start | bytes 4718596
  117.2 1.4 %copy-start.1 = (f32[2,128,512]{2,1,0:T(8,128)S(1)}, f32[2,128,512]{2,1,0:T(8,128)}, u32[]{:S(2)}) copy-start(f32[2,128,512]{2,1,0:T(8,128)} %get-tuple-element.11) | copy-start | bytes 1572868

commit v3 on v2

--- a/solution.py
+++ b/solution.py
@@ -9,7 +9,7 @@
 
 X, Z, Y = 4, 8, 4
 B, A, W = 512, 3, 128
-ROWS_A = 48
+ROWS_A = 64
 F32, BF16 = jnp.float32, jnp.bfloat16
 
 
@@ -53,10 +53,10 @@
 
 
 def kernel(
-    anc, bmap, refs_all, f1, dinv1, f2, dinv2, parent, picked,
-    cross1, diag1, cross2, diag2,
-    store, f1w, f2w, anc_v, stage, refs, low, turned, turned2, cols1, cols2, out1, out2,
-    part, dcol, dcolt, dlow, dsend1, dsend2, grow, dinv_v, dout,
+    anc, bmap_all, refs_all, f1, dinv1, f2, dinv2, parent_all, picked_all,
+    out1, diag1, out2, diag2,
+    bmap, parent, picked, store, f1w, f2w, anc_v, stage, refs, low, turned, turned2, cols1, cols2,
+    part, dcol, dcolt, dlow, dsend1, dsend2, grow, dinv_v,
     send_sems, recv_sems, local_sems,
 ):
     own, y = lax.axis_index("own"), lax.axis_index("col")
@@ -85,10 +85,17 @@
     def lanes(index):
         return pl.ds(pl.multiple_of(index * W, W), W)
 
+    barrier = pltpu.get_barrier_semaphore()
+    peers = [xup, xdn, zup, zdn, mate, ydev[1], ydev[2], ydev[3]]
+    for peer in peers:
+        pl.semaphore_signal(barrier, inc=1, device_id=peer, device_id_type=pl.DeviceIdType.MESH)
+
     load_anc = local("anc", anc, anc_v)
     load_anc.start()
-    load_refs = local("refs", refs_all.at[pl.ds(own * 2, 2)], refs)
-    load_refs.start()
+    small = [(refs_all, refs), (bmap_all, bmap), (parent_all, parent), (picked_all, picked)]
+    loads = [local(("small", i), src, dst) for i, (src, dst) in enumerate(small)]
+    for load in loads:
+        load.start()
     load_f1 = local("f1", f1, f1w.at[:, :, lanes(y), :])
     load_f1.start()
     load_f2 = local("f2", f2, f2w.at[:, :, lanes(y), :])
@@ -98,14 +105,9 @@
     load_dinv2 = local("dinv2", dinv2, dinv_v)
     load_dinv2.start()
 
-    barrier = pltpu.get_barrier_semaphore()
-    peers = [xup, xdn, zup, zdn, mate, ydev[1], ydev[2], ydev[3]]
-    for peer in peers:
-        pl.semaphore_signal(barrier, inc=1, device_id=peer, device_id_type=pl.DeviceIdType.MESH)
-    pl.semaphore_wait(barrier, len(peers))
-
     load_anc.wait()
     stage[...] = anc_v[...].astype(BF16)
+    pl.semaphore_wait(barrier, len(peers))
     mine = pl.ds(own * 2, 2)
     for d in (1, 3, 2):
         wires.send(("t", d), stage.at[:, lanes(yat(d)), :], store.at[mine, :, lanes(y)], ydev[d])
@@ -247,11 +249,12 @@
         z_wait("a", dx, 4)
     for path, dx, dz, slot in shared:
         wires.wait(("mate", path, dx, dz, slot), chunk(path, dx, dz, slot, 1), mate)
-    load_refs.wait()
+    for load in loads:
+        load.wait()
     load_f1.wait()
 
     def tile(m, i, k):
-        return store[bmap[refs[m, i, k]]]
+        return store[bmap[refs[i, k, own * 2 + m]]]
 
     def stacked(parts):
         return jnp.concatenate(parts, axis=0)
@@ -279,7 +282,7 @@
             for b in range(2):
                 turned_ref[2 * n + b, m, i] = rows[:, b * W : (b + 1) * W].T.astype(BF16)
 
-    kept1, writes = [], []
+    kept1 = []
     for m in range(2):
         for n in range(2):
             acc = 0.0
@@ -289,9 +292,6 @@
                 )
             spread(-acc, m, n, out1, turned, low)
         kept1.append(give_columns("c1", turned, cols1, m))
-        write = local(("o1", m), out1.at[m], cross1.at[m])
-        write.start()
-        writes.append(write)
 
     factor_wait("f2", f2w, False)
     factor_far("f2", f2w)
@@ -317,24 +317,26 @@
     def corrections(cols_ref, fw, m):
         return sum(dot(cols_ref[m, k], fw[m, k]) for k in range(A))
 
+    def give_rows(tag, src, dst, m):
+        for d in (1, 3, 2):
+            wires.send((tag, m, d), src.at[yat(d), m], dst.at[m, :, lanes(y)], ydev[d])
+        own_part = local((tag, m), src.at[y, m], dst.at[m, :, lanes(y)])
+        own_part.start()
+        return own_part
+
+    def take_rows(tag, dst, m, own_part):
+        own_part.wait()
+        for d in (1, 3, 2):
+            wires.wait((tag, m, d), dst.at[m, :, lanes(yat(-d))], ydev[4 - d])
+
+    kept_diag = []
     for m in range(2):
         take_columns("c1", cols1, m, kept1[m])
         turned_diag = dcolt[m] - corrections(cols1, f1w, m)
         dlow[m] = turned_diag.astype(BF16)
         for b in range(Y):
             dsend1[b, m] = turned_diag[:, b * W : (b + 1) * W].T
-
-    def give_rows(tag, src, dst):
-        for d in (1, 3, 2):
-            wires.send((tag, d), src.at[yat(d)], dst.at[:, :, lanes(y)], ydev[d])
-        own_part = local(tag, src.at[y], dst.at[:, :, lanes(y)])
-        own_part.start()
-        return own_part
-
-    def take_rows(tag, dst, own_part):
-        own_part.wait()
-        for d in (1, 3, 2):
-            wires.wait((tag, d), dst.at[:, :, lanes(yat(-d))], ydev[4 - d])
+        kept_diag.append(give_rows("g1", dsend1, diag1, m))
 
     kept2 = []
     for m in range(2):
@@ -347,56 +349,59 @@
             acc += stacked([top, part[m, :, span]])
             spread(-acc, m, n, out2, turned2, None)
         kept2.append(give_columns("c2", turned2, cols2, m))
-        write = local(("o2", m), out2.at[m], cross2.at[m])
-        write.start()
-        writes.append(write)
-    kept_diag = give_rows("g1", dsend1, diag1)
     load_dinv2.wait()
+    kept_grow = []
     for m in range(2):
         take_columns("c2", cols2, m, kept2[m])
         correction = corrections(cols2, f2w, m)
         for b in range(Y):
             dsend2[b, m] = correction[:, b * W : (b + 1) * W].T
-    kept_grow = give_rows("g2", dsend2, grow)
-    take_rows("g1", diag1, kept_diag)
-    take_rows("g2", grow, kept_grow)
-    dout[...] = dinv_v[...] - grow[...]
-    write = local("o3", dout, diag2)
-    write.start()
-    writes.append(write)
-    for write in writes:
-        write.wait()
+        kept_grow.append(give_rows("g2", dsend2, grow, m))
+    for m in range(2):
+        take_rows("g1", diag1, m, kept_diag[m])
+    for m in range(2):
+        take_rows("g2", grow, m, kept_grow[m])
+        diag2[m] = dinv_v[m] - grow[m]
     wires.finish()
+
+
+def write_out(*refs):
+    sources, results, sems = refs[:4], refs[4:8], refs[8]
+    copies = [pltpu.make_async_copy(a, b, sems.at[i]) for i, (a, b) in enumerate(zip(sources, results))]
+    for copy in copies:
+        copy.start()
+    for copy in copies:
+        copy.wait()
 
 
 def per_device(anc_store, block_map, anc_refs, factor1, dinv1, factor2, dinv2, parent, picked):
     any_space = pl.BlockSpec(memory_space=pl.ANY)
-    smem = pl.BlockSpec(memory_space=pltpu.SMEM)
+    vmem = pl.BlockSpec(memory_space=pltpu.VMEM)
+    operands = (
+        anc_store, block_map, anc_refs.transpose(1, 2, 0), factor1, dinv1, factor2, dinv2, parent, picked
+    )
     flops = 2 * 2 * 2 * (9 + 3) * W * B * B
-    return pl.pallas_call(
+    shapes = ((2, A, W, B), (2, W, B), (2, A, W, B), (2, W, B))
+    results = pl.pallas_call(
         kernel,
-        out_shape=(
-            jax.ShapeDtypeStruct((2, A, W, B), F32),
-            jax.ShapeDtypeStruct((2, W, B), F32),
-            jax.ShapeDtypeStruct((2, A, W, B), F32),
-            jax.ShapeDtypeStruct((2, W, B), F32),
-        ),
-        in_specs=[any_space, smem, any_space, any_space, any_space, any_space, any_space, smem, smem],
-        out_specs=(any_space,) * 4,
+        out_shape=tuple(pltpu.VMEM(shape, F32) for shape in shapes),
+        in_specs=[any_space] * 9,
+        out_specs=(vmem,) * 4,
         scratch_shapes=[
+            pltpu.SMEM((2 * X * Z * 2,), jnp.int32),
+            pltpu.SMEM((2,), jnp.int32),
+            pltpu.SMEM((2, 2), jnp.int32),
             pltpu.VMEM((X * Z * 4, W, B), BF16),
             pltpu.VMEM((2, A, B, B), BF16),
             pltpu.VMEM((2, A, B, B), BF16),
             pltpu.VMEM((2, B, W), F32),
             pltpu.VMEM((2, B, W), BF16),
-            pltpu.SMEM((2, A, A), jnp.int32),
+            pltpu.SMEM((A, A, 2 * X * Z * 2), jnp.int32),
             pltpu.VMEM((2, A, W, B), BF16),
             pltpu.VMEM((Y, 2, A, W, W), BF16),
             pltpu.VMEM((Y, 2, A, W, W), BF16),
             pltpu.VMEM((2, A, W, B), BF16),
             pltpu.VMEM((2, A, W, B), BF16),
-            pltpu.VMEM((2, A, W, B), F32),
-            pltpu.VMEM((2, A, W, B), F32),
             pltpu.VMEM((2, 2 * W, B), F32),
             pltpu.VMEM((2, B, W), F32),
             pltpu.VMEM((2, W, B), F32),
@@ -405,16 +410,24 @@
             pltpu.VMEM((Y, 2, W, W), F32),
             pltpu.VMEM((2, W, B), F32),
             pltpu.VMEM((2, W, B), F32),
-            pltpu.VMEM((2, W, B), F32),
             pltpu.SemaphoreType.DMA((WIRES,)),
             pltpu.SemaphoreType.DMA((WIRES,)),
             pltpu.SemaphoreType.DMA((32,)),
         ],
         compiler_params=pltpu.CompilerParams(
-            collective_id=0, has_side_effects=True, vmem_limit_bytes=56 * 1024 * 1024
+            collective_id=0, has_side_effects=True, vmem_limit_bytes=44 * 1024 * 1024
         ),
         cost_estimate=pl.CostEstimate(flops=flops, bytes_accessed=8 << 20, transcendentals=0),
-    )(anc_store, block_map, anc_refs, factor1, dinv1, factor2, dinv2, parent, picked)
+    )(*(pltpu.with_memory_space_constraint(operand, pltpu.HBM) for operand in operands))
+    return pl.pallas_call(
+        write_out,
+        out_shape=tuple(jax.ShapeDtypeStruct(shape, F32) for shape in shapes),
+        in_specs=[vmem] * 4,
+        out_specs=(any_space,) * 4,
+        scratch_shapes=[pltpu.SemaphoreType.DMA((4,))],
+        compiler_params=pltpu.CompilerParams(vmem_limit_bytes=4 * 1024 * 1024),
+        cost_estimate=pl.CostEstimate(flops=0, bytes_accessed=8 << 20, transcendentals=0),
+    )(*(pltpu.with_memory_space_constraint(result, pltpu.VMEM) for result in results))
 
 
 def solution(mesh):

time: 120 us -> 107 us (0.89)
  local copies, waits for them, and re-layouts: 7.44 us -> 0 us
  Pallas kernels: 111 us -> 106 us
    unnamed x11 -> x0, local copies, waits for them, and re-layouts: 7.44 us -> none
    pallas_call x1 -> x2, Pallas kernels: 111 us -> 106 us  [the longest x1 104 us: per_device(): pl.pallas_call(kernel, out_shape=tuple((pltpu.VMEM(shape, F32) for shape...]
where the time goes in v3:
time: 107 us
  Pallas kernels  106 us (99%)
    pallas_call x1, Pallas kernels, per_device(): pl.pallas_call(kernel, out_shape=tuple((pltpu.VMEM(shape, F32) for shape...  104 us

profile of v3, /device:TPU:1, one launch (start us, length us, event | category | flops | bytes accessed | tf_op | source)
XLA Modules:
  0.0 106.6 jit_solution(6387069100203475659)
XLA Ops:
  0.6 103.9 %shard_map.120 = (f32[2,3,128,512]{3,2,1,0:T(8,128)S(1)}, f32[2,128,512]{2,1,0:T(8,128)S(1)}, f32[2,3,128,512]{3,2,1,0:T(8,128)S(1)}, f32[2,128,512]{2,1,0:T(8,128)S(1)}) custom-call(f32[2,512,128]{2,1,0:T(8,128)} %anc.1, s32[128]{0:T(128)} %bmap_all.1, s32[3,3,128]{2,1,0:T(4,128)} %bitcast.1, bf16[2,3,128,512]{3,2,1,0:T(8,128)(2,1)} %f1.1, ...), custom_call_target="tpu_custom_call" | custom-call | flops 3221225472 | bytes 8388608 | tf_op jit(solution)/shard_map/pallas_call | solution.py:385
  104.6 2.0 %shard_map.121 = (f32[2,3,128,512]{3,2,1,0:T(8,128)}, f32[2,128,512]{2,1,0:T(8,128)}, f32[2,3,128,512]{3,2,1,0:T(8,128)}, f32[2,128,512]{2,1,0:T(8,128)}) custom-call(f32[2,3,128,512]{3,2,1,0:T(8,128)S(1)} %get-tuple-element.8.refs_0_, f32[2,128,512]{2,1,0:T(8,128)S(1)} %get-tuple-element.9.refs_1_, f32[2,3,128,512]{3,2,1,0:T(8,128)S(1)} %get-tuple-element.10.refs_2_, ...), custom_call_target="tpu_custom_call" | custom-call | bytes 8388608 | tf_op jit(solution)/shard_map/pallas_call | solution.py:422

commit v4 on v3

--- a/solution.py
+++ b/solution.py
@@ -9,8 +9,19 @@
 
 X, Z, Y = 4, 8, 4
 B, A, W = 512, 3, 128
-ROWS_A = 64
+ROWS_A = 48
 F32, BF16 = jnp.float32, jnp.bfloat16
+ORDER = (
+    ("x", "a", 0, 1), ("z", "b", 0, 1), ("f", "1", 0, 1), ("x", "b", 0, 1), ("z", "a", 0, 1),
+    ("x", "a", 0, 2), ("z", "a", -1, 1), ("z", "a", 1, 1), ("x", "b", -1, 1), ("z", "b", 0, 2),
+    ("x", "b", 1, 1), ("f", "1", 0, 2), ("x", "b", 0, 2), ("z", "a", 0, 2), ("x", "b", -1, 2),
+    ("z", "a", 2, 1), ("z", "a", -1, 2), ("x", "b", -2, 1), ("z", "a", 1, 2), ("x", "b", 2, 1),
+    ("z", "b", 0, 3), ("f", "1", 0, 3), ("x", "b", 1, 2), ("z", "a", 0, 3), ("x", "b", -2, 2),
+    ("x", "b", 2, 2), ("z", "a", 2, 2), ("z", "a", -1, 3), ("x", "b", -3, 1), ("f", "2", 0, 1),
+    ("z", "a", 1, 3), ("z", "b", 0, 4), ("x", "b", 3, 1), ("z", "a", 0, 4), ("x", "b", -3, 2),
+    ("z", "a", 2, 3), ("z", "a", -1, 4), ("z", "a", 1, 4), ("x", "b", 4, 1), ("z", "a", 2, 4),
+    ("x", "b", 3, 2), ("x", "b", 4, 2),
+)
 
 
 class Wires:
@@ -55,8 +66,8 @@
 def kernel(
     anc, bmap_all, refs_all, f1, dinv1, f2, dinv2, parent_all, picked_all,
     out1, diag1, out2, diag2,
-    bmap, parent, picked, store, f1w, f2w, anc_v, stage, refs, low, turned, turned2, cols1, cols2,
-    part, dcol, dcolt, dlow, dsend1, dsend2, grow, dinv_v,
+    bmap, parent, picked, store, f1w, f2w, anc_v, stage, refs, low, low2, turned, cols1, part,
+    dinv1_v, dinv2_v, dstage, dcolt, dlow, f2t, gsend, grow1, psum, psend, grow2,
     send_sems, recv_sems, local_sems,
 ):
     own, y = lax.axis_index("own"), lax.axis_index("col")
@@ -100,9 +111,9 @@
     load_f1.start()
     load_f2 = local("f2", f2, f2w.at[:, :, lanes(y), :])
     load_f2.start()
-    load_dcol = local("dcol", dinv1.at[:, :, lanes(y)], dcol.at[:, lanes(y), :])
-    load_dcol.start()
-    load_dinv2 = local("dinv2", dinv2, dinv_v)
+    load_dinv1 = local("dinv1", dinv1, dinv1_v)
+    load_dinv1.start()
+    load_dinv2 = local("dinv2", dinv2, dinv2_v)
     load_dinv2.start()
 
     load_anc.wait()
@@ -131,6 +142,15 @@
         wires.wait((tag, "dn", "far"), dst.at[1, :, lanes(yat(2)), :], ydev[1])
 
     factor_own("f1", f1, f1w)
+
+    load_dinv1.wait()
+    for m in range(2):
+        for b in range(Y):
+            dstage[b, m] = dinv1_v[m, :, b * W : (b + 1) * W].T.astype(BF16)
+    for d in (1, 3, 2):
+        wires.send(("d", d), dstage.at[yat(d)], dcolt.at[:, :, lanes(y)], ydev[d])
+    keep_d = local("d", dstage.at[y], dcolt.at[:, :, lanes(y)])
+    keep_d.start()
 
     keep.wait()
     for d in (1, 3, 2):
@@ -204,49 +224,24 @@
     share("a", 0, 0)
     share("b", 0, 0)
 
-    x_wait("a", 0)
-    z_wait("b", 0, 1)
-    x_wait("b", 0)
-    z_wait("a", 0, 1)
-    x_far("a", 0)
-    z_wait("b", 0, 2)
-    x_far("b", 0)
-    factor_wait("f1", f1w, True)
-    x_wait("b", -1)
-    z_wait("a", -1, 1)
-    x_wait("b", 1)
-    z_wait("a", 1, 1)
-    x_far("b", -1)
-    z_wait("b", 0, 3)
-    x_far("b", 1)
-    factor_wait("f1", f1w, False)
-    factor_own("f2", f2, f2w)
-    for d in (1, 3, 2):
-        wires.send(("d", d), dinv1.at[:, :, lanes(yat(d))], dcol.at[:, lanes(y), :], ydev[d])
-    z_wait("a", 2, 1)
-    x_wait("b", -2)
-    z_wait("a", 0, 2)
-    x_wait("b", 2)
-    z_wait("b", 0, 4)
-    x_far("b", -2)
-    x_far("b", 2)
-    z_wait("a", -1, 2)
-    factor_far("f1", f1w)
-    x_wait("b", -3)
-    z_wait("a", 1, 2)
-    x_wait("b", 3)
-    z_wait("a", 2, 2)
-    x_far("b", -3)
-    x_far("b", 3)
-    factor_wait("f2", f2w, True)
-    z_wait("a", 0, 3)
-    x_wait("b", 4)
-    z_wait("a", -1, 3)
-    x_far("b", 4)
-    z_wait("a", 1, 3)
-    z_wait("a", 2, 3)
-    for dx in (0, -1, 1, 2):
-        z_wait("a", dx, 4)
+    load_f2.wait()
+    for m in range(2):
+        for k in range(A):
+            f2t[m, :, k * W : (k + 1) * W] = f2w[m, k, lanes(y), :].T
+
+    for kind, tag, offset, step in ORDER:
+        if kind == "z":
+            z_wait(tag, offset, step)
+        elif kind == "x":
+            (x_wait if step == 1 else x_far)(tag, offset)
+        elif tag == "2":
+            factor_wait("f2", f2w, True)
+        elif step == 3:
+            factor_far("f1", f1w)
+        else:
+            factor_wait("f1", f1w, step == 1)
+            if step == 2:
+                factor_own("f2", f2, f2w)
     for path, dx, dz, slot in shared:
         wires.wait(("mate", path, dx, dz, slot), chunk(path, dx, dz, slot, 1), mate)
     for load in loads:
@@ -273,14 +268,14 @@
         for d in (1, 3, 2):
             wires.wait((tag, m, d), cols_ref.at[m, :, :, lanes(yat(-d))], ydev[4 - d])
 
-    def spread(acc, m, n, out_ref, turned_ref, low_ref):
-        for i in range(A):
-            rows = acc[i * W : (i + 1) * W]
+    def spread(acc, m, first, n, out_ref, low_ref, turned_ref=None):
+        for i in range(first, first + acc.shape[0] // W):
+            rows = acc[(i - first) * W : (i - first + 1) * W]
             out_ref[m, i, :, n * 256 : (n + 1) * 256] = rows
-            if low_ref is not None:
-                low_ref[m, i, :, n * 256 : (n + 1) * 256] = rows.astype(BF16)
-            for b in range(2):
-                turned_ref[2 * n + b, m, i] = rows[:, b * W : (b + 1) * W].T.astype(BF16)
+            low_ref[m, i, :, n * 256 : (n + 1) * 256] = rows.astype(BF16)
+            if turned_ref is not None:
+                for b in range(2):
+                    turned_ref[2 * n + b, m, i] = rows[:, b * W : (b + 1) * W].T.astype(BF16)
 
     kept1 = []
     for m in range(2):
@@ -290,29 +285,24 @@
                 acc += dot(
                     stacked([tile(m, i, k) for i in range(A)]), f1w[m, k, :, n * 256 : (n + 1) * 256]
                 )
-            spread(-acc, m, n, out1, turned, low)
+            spread(-acc, m, 0, n, out1, low, turned)
         kept1.append(give_columns("c1", turned, cols1, m))
 
     factor_wait("f2", f2w, False)
     factor_far("f2", f2w)
-    load_f2.wait()
     for m in range(2):
         p = parent[m]
         q = [picked[m, 0], picked[m, 1]]
         for n in range(2):
-            acc = 0.0
+            span = slice(n * 256, (n + 1) * 256)
+            acc = dot(stacked([low[p, q[0]], low[p, q[1]]]), f2w[m, 0, :, span])
             for k in range(2):
-                acc += dot(
-                    stacked([tile(p, q[i], q[k]) for i in range(2)]),
-                    f2w[m, k + 1, :, n * 256 : (n + 1) * 256],
-                )
-            part[m, :, n * 256 : (n + 1) * 256] = acc
-    load_dcol.wait()
+                acc += dot(stacked([tile(p, q[i], q[k]) for i in range(2)]), f2w[m, k + 1, :, span])
+            spread(-acc, m, 1, n, out2, low2)
+            part[m, :, span] = dot(f2t[m, :, W:], stacked([low2[m, 1, :, span], low2[m, 2, :, span]]))
+    keep_d.wait()
     for d in (1, 3, 2):
-        wires.wait(("d", d), dcol.at[:, lanes(yat(-d)), :], ydev[4 - d])
-    for m in range(2):
-        for b in range(Y):
-            dcolt[m, :, b * W : (b + 1) * W] = dcol[m, b * W : (b + 1) * W, :].T
+        wires.wait(("d", d), dcolt.at[:, :, lanes(yat(-d))], ydev[4 - d])
 
     def corrections(cols_ref, fw, m):
         return sum(dot(cols_ref[m, k], fw[m, k]) for k in range(A))
@@ -332,36 +322,38 @@
     kept_diag = []
     for m in range(2):
         take_columns("c1", cols1, m, kept1[m])
-        turned_diag = dcolt[m] - corrections(cols1, f1w, m)
-        dlow[m] = turned_diag.astype(BF16)
+        turned_diag = corrections(cols1, f1w, m)
+        dlow[m] = (dcolt[m].astype(F32) - turned_diag).astype(BF16)
         for b in range(Y):
-            dsend1[b, m] = turned_diag[:, b * W : (b + 1) * W].T
-        kept_diag.append(give_rows("g1", dsend1, diag1, m))
-
-    kept2 = []
+            gsend[b, m] = turned_diag[:, b * W : (b + 1) * W].T.astype(BF16)
+        kept_diag.append(give_rows("g1", gsend, grow1, m))
+
     for m in range(2):
         p = parent[m]
         q = [picked[m, 0], picked[m, 1]]
         for n in range(2):
             span = slice(n * 256, (n + 1) * 256)
-            acc = dot(stacked([dlow[p], low[p, q[0]], low[p, q[1]]]), f2w[m, 0, :, span])
-            top = dot(cols1[p, q[0]], f2w[m, 1, :, span]) + dot(cols1[p, q[1]], f2w[m, 2, :, span])
-            acc += stacked([top, part[m, :, span]])
-            spread(-acc, m, n, out2, turned2, None)
-        kept2.append(give_columns("c2", turned2, cols2, m))
+            acc = dot(dlow[p], f2w[m, 0, :, span])
+            acc += dot(cols1[p, q[0]], f2w[m, 1, :, span]) + dot(cols1[p, q[1]], f2w[m, 2, :, span])
+            spread(-acc, m, 0, n, out2, low2)
+            term = part[m, :, span] + dot(f2t[m, :, :W], low2[m, 0, :, span])
+            for b in range(Y):
+                rows = term[b * W : (b + 1) * W]
+                psum[m, b, :, span] = rows
+                psend[m, b, :, span] = rows.astype(BF16)
+        for d in (1, 3, 2):
+            wires.send(("g2", m, d), psend.at[m, yat(d)], grow2.at[m, d - 1], ydev[d])
+    for m in range(2):
+        take_rows("g1", grow1, m, kept_diag[m])
+        diag1[m] = dinv1_v[m] - grow1[m].astype(F32)
     load_dinv2.wait()
-    kept_grow = []
-    for m in range(2):
-        take_columns("c2", cols2, m, kept2[m])
-        correction = corrections(cols2, f2w, m)
-        for b in range(Y):
-            dsend2[b, m] = correction[:, b * W : (b + 1) * W].T
-        kept_grow.append(give_rows("g2", dsend2, grow, m))
-    for m in range(2):
-        take_rows("g1", diag1, m, kept_diag[m])
-    for m in range(2):
-        take_rows("g2", grow, m, kept_grow[m])
-        diag2[m] = dinv_v[m] - grow[m]
+    for m in range(2):
+        total = psum[m, y]
+        for d in (1, 3, 2):
+            wires.wait(("g2", m, d), grow2.at[m, d - 1], ydev[4 - d])
+        for d in (1, 2, 3):
+            total += grow2[m, d - 1].astype(F32)
+        diag2[m] = dinv2_v[m] - total
     wires.finish()
 
 
@@ -398,18 +390,21 @@
             pltpu.VMEM((2, B, W), BF16),
             pltpu.SMEM((A, A, 2 * X * Z * 2), jnp.int32),
             pltpu.VMEM((2, A, W, B), BF16),
-            pltpu.VMEM((Y, 2, A, W, W), BF16),
+            pltpu.VMEM((2, A, W, B), BF16),
             pltpu.VMEM((Y, 2, A, W, W), BF16),
             pltpu.VMEM((2, A, W, B), BF16),
-            pltpu.VMEM((2, A, W, B), BF16),
-            pltpu.VMEM((2, 2 * W, B), F32),
-            pltpu.VMEM((2, B, W), F32),
-            pltpu.VMEM((2, W, B), F32),
-            pltpu.VMEM((2, W, B), BF16),
-            pltpu.VMEM((Y, 2, W, W), F32),
-            pltpu.VMEM((Y, 2, W, W), F32),
+            pltpu.VMEM((2, B, B), F32),
             pltpu.VMEM((2, W, B), F32),
             pltpu.VMEM((2, W, B), F32),
+            pltpu.VMEM((Y, 2, W, W), BF16),
+            pltpu.VMEM((2, W, B), BF16),
+            pltpu.VMEM((2, W, B), BF16),
+            pltpu.VMEM((2, B, A * W), BF16),
+            pltpu.VMEM((Y, 2, W, W), BF16),
+            pltpu.VMEM((2, W, B), BF16),
+            pltpu.VMEM((2, Y, W, B), F32),
+            pltpu.VMEM((2, Y, W, B), BF16),
+            pltpu.VMEM((2, 3, W, B), BF16),
             pltpu.SemaphoreType.DMA((WIRES,)),
             pltpu.SemaphoreType.DMA((WIRES,)),
             pltpu.SemaphoreType.DMA((32,)),

time: 107 us -> 99.3 us (0.928)
  Pallas kernels: 106 us -> 98.6 us
    pallas_call x1, Pallas kernels: 104 us -> 96.5 us  [per_device(): pl.pallas_call(kernel, out_shape=tuple((pltpu.VMEM(shape, F32) for shape...]
where the time goes in v4:
time: 99.3 us; the launch traced here: 99.2 us
  Pallas kernels  98.6 us (99%)
    pallas_call x1, Pallas kernels, per_device(): pl.pallas_call(kernel, out_shape=tuple((pltpu.VMEM(shape, F32) for shape...  96.5 us
    pallas_call x1, Pallas kernels, per_device(): pl.pallas_call(write_out, out_shape=tuple((jax.ShapeDtypeStruct(shape, F3...  2.04 us

profile of v4, /device:TPU:1, one launch (start us, length us, event | category | flops | bytes accessed | tf_op | source)
XLA Modules:
  0.0 99.2 jit_solution(15102668551940550698)
XLA Ops:
  0.6 96.5 %shard_map.120 = (f32[2,3,128,512]{3,2,1,0:T(8,128)S(1)}, f32[2,128,512]{2,1,0:T(8,128)S(1)}, f32[2,3,128,512]{3,2,1,0:T(8,128)S(1)}, f32[2,128,512]{2,1,0:T(8,128)S(1)}) custom-call(f32[2,512,128]{2,1,0:T(8,128)} %anc.1, s32[128]{0:T(128)} %bmap_all.1, s32[3,3,128]{2,1,0:T(4,128)} %bitcast.1, bf16[2,3,128,512]{3,2,1,0:T(8,128)(2,1)} %f1.1, ...), custom_call_target="tpu_custom_call" | custom-call | flops 3221225472 | bytes 8388608 | tf_op jit(solution)/shard_map/pallas_call | solution.py:377
  97.2 2.0 %shard_map.121 = (f32[2,3,128,512]{3,2,1,0:T(8,128)}, f32[2,128,512]{2,1,0:T(8,128)}, f32[2,3,128,512]{3,2,1,0:T(8,128)}, f32[2,128,512]{2,1,0:T(8,128)}) custom-call(f32[2,3,128,512]{3,2,1,0:T(8,128)S(1)} %get-tuple-element.8.refs_0_, f32[2,128,512]{2,1,0:T(8,128)S(1)} %get-tuple-element.9.refs_1_, f32[2,3,128,512]{3,2,1,0:T(8,128)S(1)} %get-tuple-element.10.refs_2_, ...), custom_call_target="tpu_custom_call" | custom-call | bytes 8388608 | tf_op jit(solution)/shard_map/pallas_call | solution.py:417

commit v5 on v4

--- a/solution.py
+++ b/solution.py
@@ -12,12 +12,12 @@
 ROWS_A = 48
 F32, BF16 = jnp.float32, jnp.bfloat16
 ORDER = (
-    ("x", "a", 0, 1), ("z", "b", 0, 1), ("f", "1", 0, 1), ("x", "b", 0, 1), ("z", "a", 0, 1),
-    ("x", "a", 0, 2), ("z", "a", -1, 1), ("z", "a", 1, 1), ("x", "b", -1, 1), ("z", "b", 0, 2),
-    ("x", "b", 1, 1), ("f", "1", 0, 2), ("x", "b", 0, 2), ("z", "a", 0, 2), ("x", "b", -1, 2),
+    ("x", "a", 0, 1), ("z", "b", 0, 1), ("x", "b", 0, 1), ("z", "a", 0, 1), ("x", "a", 0, 2),
+    ("z", "a", -1, 1), ("f", "1", 0, 1), ("z", "a", 1, 1), ("x", "b", -1, 1), ("z", "b", 0, 2),
+    ("x", "b", 1, 1), ("x", "b", 0, 2), ("f", "1", 0, 2), ("z", "a", 0, 2), ("x", "b", -1, 2),
     ("z", "a", 2, 1), ("z", "a", -1, 2), ("x", "b", -2, 1), ("z", "a", 1, 2), ("x", "b", 2, 1),
-    ("z", "b", 0, 3), ("f", "1", 0, 3), ("x", "b", 1, 2), ("z", "a", 0, 3), ("x", "b", -2, 2),
-    ("x", "b", 2, 2), ("z", "a", 2, 2), ("z", "a", -1, 3), ("x", "b", -3, 1), ("f", "2", 0, 1),
+    ("z", "b", 0, 3), ("x", "b", 1, 2), ("f", "1", 0, 3), ("z", "a", 0, 3), ("x", "b", -2, 2),
+    ("x", "b", 2, 2), ("z", "a", 2, 2), ("z", "a", -1, 3), ("f", "2", 0, 1), ("x", "b", -3, 1),
     ("z", "a", 1, 3), ("z", "b", 0, 4), ("x", "b", 3, 1), ("z", "a", 0, 4), ("x", "b", -3, 2),
     ("z", "a", 2, 3), ("z", "a", -1, 4), ("z", "a", 1, 4), ("x", "b", 4, 1), ("z", "a", 2, 4),
     ("x", "b", 3, 2), ("x", "b", 4, 2),
@@ -125,10 +125,9 @@
     keep = local("t", stage.at[:, lanes(y), :], store.at[mine, :, lanes(y)])
     keep.start()
 
-    def factor_own(tag, src, dst):
-        for m, k in ((0, 1), (1, 0)):
-            wires.send((tag, "up", m), src.at[m], dst.at[m, :, lanes(y), :], ydev[1])
-            wires.send((tag, "dn", k), src.at[k], dst.at[k, :, lanes(y), :], ydev[3])
+    def factor_own(tag, src, dst, m):
+        wires.send((tag, "up", m), src.at[m], dst.at[m, :, lanes(y), :], ydev[1])
+        wires.send((tag, "dn", 1 - m), src.at[1 - m], dst.at[1 - m, :, lanes(y), :], ydev[3])
 
     def factor_wait(tag, dst, first):
         for way, d, m in (("up", -1, 0 if first else 1), ("dn", 1, 1 if first else 0)):
@@ -141,14 +140,11 @@
         wires.wait((tag, "up", "far"), dst.at[0, :, lanes(yat(2)), :], ydev[3])
         wires.wait((tag, "dn", "far"), dst.at[1, :, lanes(yat(2)), :], ydev[1])
 
-    factor_own("f1", f1, f1w)
-
     load_dinv1.wait()
     for m in range(2):
         for b in range(Y):
             dstage[b, m] = dinv1_v[m, :, b * W : (b + 1) * W].T.astype(BF16)
-    for d in (1, 3, 2):
-        wires.send(("d", d), dstage.at[yat(d)], dcolt.at[:, :, lanes(y)], ydev[d])
+    factor_own("f1", f1, f1w, 0)
     keep_d = local("d", dstage.at[y], dcolt.at[:, :, lanes(y)])
     keep_d.start()
 
@@ -172,47 +168,49 @@
     XWAY = {"up": (xup, xdn, -1), "dn": (xdn, xup, 1)}
     SLOT = {"up": 0, "dn": 1}
 
-    def z_send(path, dx, step, slot=None):
-        for way, (to, _, sign) in ZWAY.items():
-            half = SLOT[way] if step == 4 else slot
-            piece = chunk(path, dx, sign * (step - 1), half)
-            wires.send(("z", path, dx, way, step), piece, piece, to)
+    def z_send(path, dx, step):
+        for slot in range(2):
+            for way, (to, _, sign) in ZWAY.items():
+                piece = chunk(path, dx, sign * (step - 1), slot)
+                wires.send(("z", path, dx, way, step, slot), piece, piece, to)
 
     def x_send(path, dz):
-        piece = chunk(path, 0, dz)
-        for way, (to, _, _) in XWAY.items():
-            wires.send(("x", path, dz, way, 1), piece, piece, to)
+        for slot in range(2):
+            for way, (to, _, _) in XWAY.items():
+                piece = chunk(path, 0, dz, slot)
+                wires.send(("x", path, dz, way, 1, slot), piece, piece, to)
 
     def z_wait(path, dx, step):
-        for way, (to, source, sign) in ZWAY.items():
-            half = SLOT[way] if step == 4 else None
-            piece = chunk(path, dx, sign * step, half)
-            wires.wait(("z", path, dx, way, step), piece, source)
-            if step < 4:
-                half = SLOT[way] if step == 3 else None
-                on = chunk(path, dx, sign * step, half)
-                wires.send(("z", path, dx, way, step + 1), on, on, to)
-                if path == "b":
-                    x_send("b", sign * step)
-                share(path, dx, sign * step)
-        if step == 4:
+        for slot in range(2):
+            for way, (to, source, sign) in ZWAY.items():
+                if step == 4 and slot != SLOT[way]:
+                    continue
+                piece = chunk(path, dx, sign * step, slot)
+                wires.wait(("z", path, dx, way, step, slot), piece, source)
+                if step < 3 or (step == 3 and slot == SLOT[way]):
+                    wires.send(("z", path, dx, way, step + 1, slot), piece, piece, to)
+        for way, (_, _, sign) in ZWAY.items():
+            if step == 4 and way == "dn":
+                continue
             if path == "b":
-                x_send("b", 4)
-            share(path, dx, 4)
+                x_send("b", 4 if step == 4 else sign * step)
+            share(path, dx, 4 if step == 4 else sign * step)
 
     def x_wait(path, dz):
-        for way, (to, source, sign) in XWAY.items():
-            piece = chunk(path, sign, dz)
-            wires.wait(("x", path, dz, way, 1), piece, source)
-            on = chunk(path, sign, dz, SLOT[way])
-            wires.send(("x", path, dz, way, 2), on, on, to)
+        for slot in range(2):
+            for way, (to, source, sign) in XWAY.items():
+                piece = chunk(path, sign, dz, slot)
+                wires.wait(("x", path, dz, way, 1, slot), piece, source)
+                if slot == SLOT[way]:
+                    wires.send(("x", path, dz, way, 2, slot), piece, piece, to)
+        for sign in (-1, 1):
             if path == "a":
                 z_send("a", sign, 1)
             share(path, sign, dz)
 
     def x_far(path, dz):
         for way, (_, source, _) in XWAY.items():
-            wires.wait(("x", path, dz, way, 2), chunk(path, 2, dz, SLOT[way]), source)
+            wires.wait(("x", path, dz, way, 2, SLOT[way]), chunk(path, 2, dz, SLOT[way]), source)
         if path == "a":
             z_send("a", 2, 1)
         share(path, 2, dz)
@@ -223,6 +221,7 @@
     x_send("b", 0)
     share("a", 0, 0)
     share("b", 0, 0)
+    factor_own("f1", f1, f1w, 1)
 
     load_f2.wait()
     for m in range(2):
@@ -236,12 +235,15 @@
             (x_wait if step == 1 else x_far)(tag, offset)
         elif tag == "2":
             factor_wait("f2", f2w, True)
+            for d in (1, 3, 2):
+                wires.send(("d", d), dstage.at[yat(d)], dcolt.at[:, :, lanes(y)], ydev[d])
         elif step == 3:
             factor_far("f1", f1w)
+            factor_own("f2", f2, f2w, 1)
         else:
             factor_wait("f1", f1w, step == 1)
             if step == 2:
-                factor_own("f2", f2, f2w)
+                factor_own("f2", f2, f2w, 0)
     for path, dx, dz, slot in shared:
         wires.wait(("mate", path, dx, dz, slot), chunk(path, dx, dz, slot, 1), mate)
     for load in loads:
@@ -359,7 +361,8 @@
 
 def write_out(*refs):
     sources, results, sems = refs[:4], refs[4:8], refs[8]
-    copies = [pltpu.make_async_copy(a, b, sems.at[i]) for i, (a, b) in enumerate(zip(sources, results))]
+    pairs = [(a.at[m], b.at[m]) for m in range(2) for a, b in zip(sources, results)]
+    copies = [pltpu.make_async_copy(a, b, sems.at[i]) for i, (a, b) in enumerate(pairs)]
     for copy in copies:
         copy.start()
     for copy in copies:
@@ -419,7 +422,7 @@
         out_shape=tuple(jax.ShapeDtypeStruct(shape, F32) for shape in shapes),
         in_specs=[vmem] * 4,
         out_specs=(any_space,) * 4,
-        scratch_shapes=[pltpu.SemaphoreType.DMA((4,))],
+        scratch_shapes=[pltpu.SemaphoreType.DMA((8,))],
         compiler_params=pltpu.CompilerParams(vmem_limit_bytes=4 * 1024 * 1024),
         cost_estimate=pl.CostEstimate(flops=0, bytes_accessed=8 << 20, transcendentals=0),
     )(*(pltpu.with_memory_space_constraint(result, pltpu.VMEM) for result in results))

time: 99.3 us -> 99.1 us (level)
  no operation moved by 1% of the time
where the time goes in v5:
time: 99.1 us; the launch traced here: 99 us
  Pallas kernels  98.3 us (99%)
    pallas_call x1, Pallas kernels, per_device(): pl.pallas_call(kernel, out_shape=tuple((pltpu.VMEM(shape, F32) for shape...  96.3 us
    pallas_call x1, Pallas kernels, per_device(): pl.pallas_call(write_out, out_shape=tuple((jax.ShapeDtypeStruct(shape, F3...  2.07 us

profile of v5, /device:TPU:1, one launch (start us, length us, event | category | flops | bytes accessed | tf_op | source)
XLA Modules:
  0.0 99.0 jit_solution(1287158224409949387)
XLA Ops:
  0.6 96.3 %shard_map.120 = (f32[2,3,128,512]{3,2,1,0:T(8,128)S(1)}, f32[2,128,512]{2,1,0:T(8,128)S(1)}, f32[2,3,128,512]{3,2,1,0:T(8,128)S(1)}, f32[2,128,512]{2,1,0:T(8,128)S(1)}) custom-call(f32[2,512,128]{2,1,0:T(8,128)} %anc.1, s32[128]{0:T(128)} %bmap_all.1, s32[3,3,128]{2,1,0:T(4,128)} %bitcast.1, bf16[2,3,128,512]{3,2,1,0:T(8,128)(2,1)} %f1.1, ...), custom_call_target="tpu_custom_call" | custom-call | flops 3221225472 | bytes 8388608 | tf_op jit(solution)/shard_map/pallas_call | solution.py:380
  96.9 2.1 %shard_map.121 = (f32[2,3,128,512]{3,2,1,0:T(8,128)}, f32[2,128,512]{2,1,0:T(8,128)}, f32[2,3,128,512]{3,2,1,0:T(8,128)}, f32[2,128,512]{2,1,0:T(8,128)}) custom-call(f32[2,3,128,512]{3,2,1,0:T(8,128)S(1)} %get-tuple-element.8.refs_0_, f32[2,128,512]{2,1,0:T(8,128)S(1)} %get-tuple-element.9.refs_1_, f32[2,3,128,512]{3,2,1,0:T(8,128)S(1)} %get-tuple-element.10.refs_2_, ...), custom_call_target="tpu_custom_call" | custom-call | bytes 8388608 | tf_op jit(solution)/shard_map/pallas_call | solution.py:420
